TPU v7x, 256 devices: a whole 4x4x8 slice. The times are simulated.
256 devices in a mesh: ctx: 64 (over x, z_lo, y, core), head: 4 (over z_hi).
Axes of the slice: x: 4, y: 4, z: 8 (z_hi: 4, z_lo: 2; z = z_hi * 2 + z_lo), core: 2. Of those that a mesh axis runs over, the one named last changes fastest.
Arguments:
- layer_input: bfloat16 [8192, 8192], P('ctx'), may hold values from -6 to 6
- key_weight: bfloat16 [8192, 512], P(None, 'head'), may hold values from -0.0625 to 0.0625
- value_weight: bfloat16 [8192, 512], P(None, 'head'), may hold values from -0.0625 to 0.0625
- queries: bfloat16 [8192, 4096], P('ctx', 'head'), may hold values from -160 to 160
- out_grad: bfloat16 [8192, 4096], P('ctx', 'head'), may hold values from -192 to 192
- doc_start: int32 [8192], P('ctx'), may hold values from 0 to 8191, as said below
- block_order: int32 [128], replicated, may hold values from 0 to 127, as said below
Outputs:
- input_grad: bfloat16 [8192, 8192], P('ctx', 'head')
- query_grad: bfloat16 [8192, 4096], P('ctx', 'head')
Inputs may be any that keep to these rules, and one draw needn't show every extreme that they name: `block_order`: entries 2d and 2d + 1 are j and 127 - j for some j < 64; all entries together are a permutation. doc_start of a row is the first position of the row's document, at most the row's own position; documents are runs of positions, at most 8 of them, and the last position forms a document of its own.
All inputs are finite; a program needn't handle non-finite values.
Results may differ from a plain program's by a relative error of at most 0.018.
Values may be sent and summed in bfloat16 or wider, within the bound.
No kernel may reach another device: no remote copies, remote signals or barrier semaphores. Data moves between devices by JAX's collectives and lax.ppermute only.
A program may use at most 128 MiB of HBM per device.

v0:
```python
import functools
import math

import jax
import jax.numpy as jnp
from jax import lax
from jax.experimental import pallas as pl
from jax.experimental.pallas import tpu as pltpu
from jax.sharding import Mesh
from jax.sharding import PartitionSpec as P

rope_base = 500000.0
big_negative = -1e30
n_ctx = 64
n_head = 4
block_len = 64
key_span = 256
granule = 16
item_group = 3
log2e = 1.4426950408889634


swap = [(0, 1), (1, 0)]
both_swap = [(0, 3), (1, 2), (2, 1), (3, 0)]


def head_perm(s):
    return [(h, (h + s) % n_head) for h in range(n_head)]


def rotation_tables(positions, width):
    half_width = width // 2
    exponent = jnp.arange(half_width, dtype=jnp.float32) * (2.0 / width)
    frequency = jnp.exp(-math.log(rope_base) * exponent)
    angles = positions.astype(jnp.float32)[:, None] * frequency[None, :]
    return (jnp.cos(angles), jnp.sin(angles))


def rotate(vectors, cos_table, sin_table):
    half_width = vectors.shape[1] // 2
    a = vectors[:, :half_width]
    b = vectors[:, half_width:]
    return jnp.concatenate([a * cos_table - b * sin_table, b * cos_table + a * sin_table], axis=1)


def stored_block(place_ref, x, y, rel, block):
    z_at = place_ref[2] ^ (rel // 2)
    core_at = place_ref[3] ^ (rel % 2)
    return ((x * 2 + z_at) * 4 + y) * 4 + core_at * 2 + block


def each_granule(place_ref, order_ref, visit):
    def one_node(node, carry):
        for rel in range(4):
            for block in range(2):
                stored = stored_block(place_ref, node // 4, node % 4, rel, block)
                visit(order_ref[stored], node * 8 + rel * 2 + block)
        return carry

    lax.fori_loop(0, 16, one_node, 0, unroll=2)


def granule_rows(index):
    return pl.ds(pl.multiple_of(index * granule, granule), granule)


def load_operands(place_ref, order_ref, gathered, packs, kv, q_rows, g_rows, starts):
    tokens = kv.shape[0] - key_span
    kv[tokens:, :] = jnp.zeros_like(kv[tokens:, :])

    def fetch(seq, entry):
        kv[granule_rows(seq), :] = gathered[granule_rows(entry), :]

    each_granule(place_ref, order_ref, fetch)
    head_dim = q_rows.shape[1]
    half = starts.shape[1]
    for rel in range(4):
        pack = packs[rel]
        code = pack[256:272, :].astype(jnp.float32)
        start = (code[0:1, :] * 128.0 + code[1:2, :]).astype(jnp.int32)
        for block in range(2):
            part = rel * 2 + block
            starts[part : part + 1, :] = start[:, block * half : (block + 1) * half]
            for group in range(half // block_len):
                to = pl.ds(part * half + group * block_len, block_len)
                cols = pl.ds(group * head_dim, head_dim)
                q_rows[to, :] = pack[block * block_len : (block + 1) * block_len, cols]
                g_rows[to, :] = pack[128 + block * block_len : 128 + (block + 1) * block_len, cols]


contract_last = (((1,), (1,)), ((), ()))


def part_block(place_ref, order_ref, part):
    return order_ref[stored_block(place_ref, place_ref[0], place_ref[1], part // 2, part % 2)]


def part_slot(place_ref, part):
    return ((place_ref[2] * 2 + place_ref[3]) ^ (part // 2)) * 2 + part % 2


def list_items(place_ref, order_ref, starts, items):
    filled = 0
    for part in range(8):
        block = part_block(place_ref, order_ref, part)
        first = jnp.min(starts[part : part + 1, :]) // block_len
        count = (block - first + key_span // granule) // (key_span // granule)

        def add(k, at, part=part, block=block, first=first):
            items[0, at] = part
            items[1, at] = first + k * (key_span // granule)
            items[2, at] = block * block_len
            return at + 1

        filled = lax.fori_loop(0, count, add, filled)
    for spare in range(item_group - 1):
        items[0, filled + spare] = 7
        items[1, filled + spare] = 16 * 8
        items[2, filled + spare] = 0
    return (filled + item_group - 1) // item_group


def fill_positions(key_rel):
    row = lax.broadcasted_iota(jnp.int32, key_rel.shape, 0)
    key_rel[...] = (row // granule) * block_len + row % granule


def item_terms(i, items, place_ref, kv, q_rows, g_rows, starts, key_rel, factor):
    part, first = items[0, i], items[1, i]
    half = starts.shape[1]
    head_dim = q_rows.shape[1]
    rows = pl.ds(pl.multiple_of(first * granule, granule), key_span)
    cols = pl.ds(pl.multiple_of(part * half, half), half)
    offset = first * block_len + (place_ref[2] * 2 + place_ref[3]) * granule
    key = kv[rows, : 2 * head_dim]
    value = kv[rows, 2 * head_dim :]
    q_part = q_rows[cols, :]
    g_part = g_rows[cols, :]
    score = lax.dot_general(
        key,
        jnp.concatenate([q_part, q_part], axis=1),
        contract_last,
        preferred_element_type=jnp.float32,
    )
    prob_grad = lax.dot_general(value, g_part, contract_last, preferred_element_type=jnp.float32)
    lane = lax.broadcasted_iota(jnp.int32, (1, half), 1) % block_len
    end = lane + (items[2, i] - offset)
    start = starts[pl.ds(part, 1), :] - offset
    live = (key_rel[...] <= end) & (key_rel[...] >= start)
    return part, rows, key, q_part, g_part, score * factor, prob_grad, live


def stats_kernel(place_ref, order_ref, *refs, factor):
    gathered, packs, stats_ref = refs[0], refs[1:5], refs[5]
    kv, q_rows, g_rows, starts, key_rel, items, tops, totals, weights = refs[6:]
    load_operands(place_ref, order_ref, gathered, packs, kv, q_rows, g_rows, starts)
    fill_positions(key_rel)
    tops[...] = jnp.full_like(tops, big_negative)
    totals[...] = jnp.zeros_like(totals)
    weights[...] = jnp.zeros_like(weights)
    step_count = list_items(place_ref, order_ref, starts, items)

    def one_step(step, carry):
        both = [
            item_terms(
                item_group * step + i, items, place_ref, kv, q_rows, g_rows, starts, key_rel, factor
            )
            for i in range(item_group)
        ]
        for part, _, _, _, _, score, prob_grad, live in both:
            at = pl.ds(part, 1)
            top = tops[at, :]
            score = jnp.where(live, score, big_negative)
            new_top = jnp.maximum(top, jnp.max(score, axis=0, keepdims=True))
            growth = jnp.exp2(score - new_top)
            faded = jnp.exp2(top - new_top)
            tops[at, :] = new_top
            totals[at, :] = totals[at, :] * faded + jnp.sum(growth, axis=0, keepdims=True)
            weights[at, :] = weights[at, :] * faded + jnp.sum(
                growth * prob_grad, axis=0, keepdims=True
            )
        return carry

    lax.fori_loop(0, step_count, one_step, 0)
    for part in range(8):
        slot = part_slot(place_ref, part)
        at = slice(part, part + 1)
        stats_ref[pl.ds(slot, 1), :] = tops[at, :] + jnp.log2(totals[at, :])
        stats_ref[pl.ds(8 + slot, 1), :] = weights[at, :] / totals[at, :]


def grads_kernel(place_ref, order_ref, *refs, factor, scaling):
    gathered, packs, stats = refs[0], refs[1:5], refs[5:9]
    out_ref, dq_own, dq_others = refs[9], refs[10], refs[11:14]
    kv, q_rows, g_rows, starts, key_rel, items, acc, dq_acc, logs, deltas = refs[14:24]
    out_buf, own_buf, *other_bufs, sems = refs[24:]
    dq_bufs = (own_buf, *other_bufs)
    copies = [
        pltpu.make_async_copy(buf, ref, sems.at[i])
        for i, (buf, ref) in enumerate(zip((*dq_bufs, out_buf), (dq_own, *dq_others, out_ref)))
    ]
    load_operands(place_ref, order_ref, gathered, packs, kv, q_rows, g_rows, starts)
    half = starts.shape[1]
    head_dim = q_rows.shape[1]
    acc[...] = jnp.zeros_like(acc)
    fill_positions(key_rel)

    top = jnp.maximum(
        jnp.maximum(stats[0][:8, :], stats[1][:8, :]), jnp.maximum(stats[2][:8, :], stats[3][:8, :])
    )
    total = jnp.zeros_like(top)
    weighted = jnp.zeros_like(top)
    for s in stats:
        share = jnp.exp2(s[:8, :] - top)
        total = total + share
        weighted = weighted + share * s[8:, :]
    logs[...] = top + jnp.log2(total)
    deltas[...] = weighted / total

    dq_acc[...] = jnp.zeros_like(dq_acc)
    step_count = list_items(place_ref, order_ref, starts, items)
    quarter = place_ref[2] * 2 + place_ref[3]

    def one_step(step, carry):
        both = [
            item_terms(
                item_group * step + i, items, place_ref, kv, q_rows, g_rows, starts, key_rel, factor
            )
            for i in range(item_group)
        ]
        results = []
        for part, rows, key, q_part, g_part, score, prob_grad, live in both:
            slot = pl.ds((quarter ^ (part // 2)) * 2 + part % 2, 1)
            prob = jnp.where(live, jnp.exp2(score - logs[slot, :]), 0.0)
            score_grad = (prob * ((prob_grad - deltas[slot, :]) * scaling)).astype(jnp.bfloat16)
            key_part = jnp.dot(score_grad, q_part, preferred_element_type=jnp.float32)
            value_part = jnp.dot(
                prob.astype(jnp.bfloat16), g_part, preferred_element_type=jnp.float32
            )
            query_part = jnp.dot(key.T, score_grad, preferred_element_type=jnp.float32)
            results.append((part, rows, key_part, value_part, query_part))
        for part, rows, key_part, value_part, query_part in results:
            acc[rows, :head_dim] += key_part
            acc[rows, head_dim:] += value_part
            at = pl.ds(pl.multiple_of(part * head_dim, head_dim), head_dim)
            dq_acc[at, :] += query_part[:head_dim, :] + query_part[head_dim:, :]
        return carry

    lax.fori_loop(0, step_count, one_step, 0)
    for part in range(8):
        dq = dq_acc[part * head_dim : (part + 1) * head_dim, :].T
        rel, block = part // 2, part % 2
        buf = dq_bufs[rel]
        for group in range(half // block_len):
            buf[block * block_len : (block + 1) * block_len, pl.ds(group * head_dim, head_dim)] = (
                dq[group * block_len : (group + 1) * block_len, :].astype(buf.dtype)
            )
        if block == 1:
            copies[rel].start()

    def store(seq, entry):
        out_buf[granule_rows(entry), :] = acc[granule_rows(seq), :].astype(jnp.bfloat16)

    each_granule(place_ref, order_ref, store)
    copies[4].start()
    for copy in copies:
        copy.wait()


def kernel_scratch(quarter, head_dim, rows):
    half = rows // 2
    return [
        pltpu.VMEM((quarter + key_span, 3 * head_dim), jnp.bfloat16),
        pltpu.VMEM((4 * rows, head_dim), jnp.bfloat16),
        pltpu.VMEM((4 * rows, head_dim), jnp.bfloat16),
        pltpu.VMEM((8, half), jnp.int32),
        pltpu.VMEM((key_span, half), jnp.int32),
        pltpu.SMEM((3, 64), jnp.int32),
    ]


def run_stats(place, order, gathered, packs, scaling, tokens, head_dim, rows):
    smem = pl.BlockSpec(memory_space=pltpu.SMEM)
    vmem = pl.BlockSpec(memory_space=pltpu.VMEM)
    return pl.pallas_call(
        functools.partial(stats_kernel, factor=scaling * log2e),
        out_shape=jax.ShapeDtypeStruct((16, rows // 2), jnp.float32),
        in_specs=[smem, smem] + [vmem] * 5,
        out_specs=vmem,
        scratch_shapes=kernel_scratch(tokens // 4, head_dim, rows)
        + [pltpu.VMEM((8, rows // 2), jnp.float32)] * 3,
        compiler_params=pltpu.CompilerParams(vmem_limit_bytes=32 * 1024 * 1024),
        cost_estimate=pl.CostEstimate(
            flops=8 * rows * tokens * head_dim,
            bytes_accessed=4 * 1024 * 1024,
            transcendentals=rows * tokens // 2,
        ),
    )(place, order, gathered, *packs)


def run_grads(place, order, gathered, packs, stats, scaling, tokens, head_dim, rows):
    smem = pl.BlockSpec(memory_space=pltpu.SMEM)
    vmem = pl.BlockSpec(memory_space=pltpu.VMEM)
    quarter = tokens // 4
    half = rows // 2
    return pl.pallas_call(
        functools.partial(grads_kernel, factor=scaling * log2e, scaling=scaling),
        out_shape=[
            jax.ShapeDtypeStruct((quarter, 2 * head_dim), jnp.bfloat16),
            jax.ShapeDtypeStruct((2 * block_len, (half // block_len) * head_dim), jnp.float32),
        ]
        + [jax.ShapeDtypeStruct((2 * block_len, (half // block_len) * head_dim), jnp.bfloat16)] * 3,
        in_specs=[smem, smem] + [vmem] * 9,
        out_specs=[pl.BlockSpec(memory_space=pltpu.HBM)] * 5,
        scratch_shapes=kernel_scratch(quarter, head_dim, rows)
        + [
            pltpu.VMEM((quarter + key_span, 2 * head_dim), jnp.float32),
            pltpu.VMEM((8 * head_dim, half), jnp.float32),
            pltpu.VMEM((8, half), jnp.float32),
            pltpu.VMEM((8, half), jnp.float32),
            pltpu.VMEM((quarter, 2 * head_dim), jnp.bfloat16),
            pltpu.VMEM((2 * block_len, (half // block_len) * head_dim), jnp.float32),
        ]
        + [pltpu.VMEM((2 * block_len, (half // block_len) * head_dim), jnp.bfloat16)] * 3
        + [pltpu.SemaphoreType.DMA((5,))],
        compiler_params=pltpu.CompilerParams(vmem_limit_bytes=57 * 1024 * 1024),
        cost_estimate=pl.CostEstimate(
            flops=16 * rows * tokens * head_dim,
            bytes_accessed=8 * 1024 * 1024,
            transcendentals=rows * tokens // 2,
        ),
    )(place, order, gathered, *packs, *stats)


def finish_kernel(place_ref, parts_ref, cos_ref, sin_ref, out_ref):
    head_dim = cos_ref.shape[1]
    rows = out_ref.shape[1]
    for rel in range(4):
        at = pl.ds(rel * rows, rows)
        total = parts_ref[0, at, :].astype(jnp.float32)
        for i in range(1, parts_ref.shape[0]):
            total += parts_ref[i, at, :].astype(jnp.float32)
        key = total[:, :head_dim]
        key = key * cos_ref[at, :] + pltpu.roll(key, head_dim // 2, 1) * sin_ref[at, :]
        back = jnp.concatenate([key, total[:, head_dim:]], axis=1).astype(jnp.bfloat16)
        owner = (place_ref[0] ^ rel) * n_head
        for head in range(n_head):
            out_ref[owner + head] = back


def run_finish(place, parts, cos_wide, sin_wide):
    smem = pl.BlockSpec(memory_space=pltpu.SMEM)
    vmem = pl.BlockSpec(memory_space=pltpu.VMEM)
    _, rows, width = parts.shape
    return pl.pallas_call(
        finish_kernel,
        out_shape=jax.ShapeDtypeStruct((4 * n_head, rows // 4, width), jnp.bfloat16),
        in_specs=[smem] + [vmem] * 3,
        out_specs=vmem,
        compiler_params=pltpu.CompilerParams(vmem_limit_bytes=16 * 1024 * 1024),
        cost_estimate=pl.CostEstimate(
            flops=20 * rows * width, bytes_accessed=2 * 1024 * 1024, transcendentals=0
        ),
    )(place, parts, cos_wide, sin_wide)


def product_kernel(place_ref, back_ref, mine_ref, other_ref, out_ref, left_mine, left_other):
    head_dim = back_ref.shape[2] // 2
    first = pl.multiple_of(place_ref[1] * head_dim, head_dim)
    second = pl.multiple_of(head_dim - first, head_dim)
    for source in range(back_ref.shape[0]):
        quarter, shift = source // n_head, source % n_head
        sender = quarter * n_head + (place_ref[2] + n_head - shift) % n_head
        cols = pl.ds(shift * head_dim, head_dim)
        for block in range(2):
            to = pl.ds(block * block_len + quarter * granule, granule)
            at = pl.ds(block * granule, granule)
            left_mine[to, cols] = back_ref[sender, at, pl.ds(first, head_dim)]
            left_other[to, cols] = back_ref[sender, at, pl.ds(second, head_dim)]
    for tile in range(out_ref.shape[1] // 512):
        at = pl.ds(tile * 512, 512)
        total = lax.dot_general(
            left_mine[...], mine_ref[at, :], contract_last, preferred_element_type=jnp.float32
        )
        total += lax.dot_general(
            left_other[...], other_ref[at, :], contract_last, preferred_element_type=jnp.float32
        )
        out_ref[:, at] = total.astype(jnp.bfloat16)


def run_product(place, back, mine, other):
    smem = pl.BlockSpec(memory_space=pltpu.SMEM)
    vmem = pl.BlockSpec(memory_space=pltpu.VMEM)
    row_count = back.shape[0] * back.shape[1] // n_head
    out_width, depth = mine.shape
    return pl.pallas_call(
        product_kernel,
        out_shape=jax.ShapeDtypeStruct((row_count, out_width), jnp.bfloat16),
        in_specs=[smem] + [vmem] * 3,
        out_specs=vmem,
        scratch_shapes=[pltpu.VMEM((row_count, depth), jnp.bfloat16)] * 2,
        compiler_params=pltpu.CompilerParams(vmem_limit_bytes=24 * 1024 * 1024),
        cost_estimate=pl.CostEstimate(
            flops=4 * row_count * depth * out_width,
            bytes_accessed=5 * 1024 * 1024,
            transcendentals=0,
        ),
    )(place, back, mine, other)


def shards(layer_input, key_weight, value_weight, queries, out_grad, doc_start, block_order):
    f32, bf16 = jnp.float32, jnp.bfloat16
    row_count = layer_input.shape[0]
    tokens = row_count * n_ctx
    head_dim = key_weight.shape[1]
    width = key_weight.shape[0]
    groups = queries.shape[1] // head_dim
    rows = row_count * groups
    scaling = 1.0 / math.sqrt(head_dim)
    x, y = lax.axis_index("x"), lax.axis_index("y")
    z, core, head = lax.axis_index("zl"), lax.axis_index("core"), lax.axis_index("head")
    core_is_one = core == 1

    def pick(v, index, axis):
        return lax.dynamic_index_in_dim(v, index, axis, keepdims=False)

    def blocks_of(z_at, core_at):
        at = ((x * 2 + z_at) * 4 + y) * 4 + core_at * 2
        return lax.dynamic_slice_in_dim(block_order, at, 2)

    own_blocks = blocks_of(z, core)
    own_pos = (
        own_blocks[:, None] * block_len + jnp.arange(block_len, dtype=jnp.int32)[None, :]
    ).reshape(-1)
    cos_own, sin_own = rotation_tables(own_pos, head_dim)
    key_raw = jnp.dot(layer_input, key_weight, preferred_element_type=f32)
    keys = rotate(key_raw, cos_own, sin_own)
    key_hi = lax.reduce_precision(keys, 8, 7)
    key_lo = keys - key_hi
    values = jnp.dot(layer_input, value_weight, preferred_element_type=f32)
    local = jnp.concatenate(
        [key_hi.astype(bf16), key_lo.astype(bf16), values.astype(bf16)], axis=1
    ).reshape(2, 2, 2, granule, 3 * head_dim)

    pair = jnp.stack(
        [pick(local, core, 2), lax.ppermute(pick(local, 1 - core, 2), "core", swap)]
    )

    node = jnp.stack([pick(pair, z, 2), lax.ppermute(pick(pair, 1 - z, 2), "zl", swap)])
    node = node.reshape(1, row_count, 3 * head_dim)

    out_width = width // n_head
    share = out_width // 16
    node_index = x * 4 + y

    def weight_share(w):
        return pick(w.reshape(n_head, 16, share, head_dim), node_index, 1)

    weight_shares = jnp.where(
        core_is_one, weight_share(value_weight), weight_share(key_weight)
    )
    node, weight_shares = lax.optimization_barrier((node, weight_shares))
    weight_rows = [pick(weight_shares, head, 0)] + [
        lax.ppermute(pick(weight_shares, (head + s) % n_head, 0), "head", head_perm(s))
        for s in (1, 2, 3)
    ]
    weight_rows = jnp.concatenate(weight_rows, axis=1)[None]
    weight_rows = jnp.broadcast_to(weight_rows, (16, share, n_head * head_dim))

    def per_column(v):
        return jnp.broadcast_to(v.reshape(2, 1, block_len), (2, groups, block_len)).reshape(1, rows)

    start_cols = per_column(doc_start)
    start_code = jnp.concatenate(
        [start_cols // 128, start_cols % 128, jnp.zeros((14, rows), jnp.int32)], axis=0
    ).astype(bf16)
    pack_own = jnp.concatenate([queries, out_grad, start_code], axis=0)
    pack_z = lax.ppermute(pack_own, "zl", swap)
    pack_z, weight_rows = lax.optimization_barrier((pack_z, weight_rows))
    packs = [
        pack_own,
        lax.ppermute(pack_own, "core", swap),
        pack_z,
        lax.ppermute(pack_z, "core", swap),
    ]

    gathered = lax.all_to_all(
        jnp.broadcast_to(node, (16, row_count, 3 * head_dim)), ("x", "y"), 0, 0
    ).reshape(tokens // 4, 3 * head_dim)
    weights_mine = lax.all_to_all(weight_rows, ("x", "y"), 0, 0)

    quarter = z * 2 + core
    place = jnp.stack([x, y, z, core]).astype(jnp.int32)
    stats = run_stats(place, block_order, gathered, packs, scaling, tokens, head_dim, rows)
    stats_all = [
        stats,
        lax.ppermute(stats, "core", swap),
        lax.ppermute(stats, "zl", swap),
        lax.ppermute(stats, ("zl", "core"), both_swap),
    ]
    grads, dq_own, *dq_others = run_grads(
        place, block_order, gathered, packs, stats_all, scaling, tokens, head_dim, rows
    )
    grads, weights_mine = lax.optimization_barrier((grads, weights_mine))
    weights_mine = weights_mine.reshape(out_width, n_head * head_dim)
    weights_other = lax.ppermute(weights_mine, "core", swap)

    grads = lax.all_to_all(
        grads.reshape(16, row_count, 2 * head_dim), ("x", "y"), 0, 0
    )
    node_blocks = jnp.concatenate(
        [blocks_of(z ^ (rel // 2), core ^ (rel % 2)) for rel in range(4)]
    )
    quarter_pos = (
        node_blocks[:, None] * block_len
        + quarter * granule
        + jnp.arange(granule, dtype=jnp.int32)[None, :]
    ).reshape(-1)
    cos_node, sin_node = rotation_tables(quarter_pos, head_dim)

    here = jnp.stack([quarter, core, head]).astype(jnp.int32)
    back = run_finish(
        here,
        grads,
        jnp.concatenate([cos_node, cos_node], axis=1),
        jnp.concatenate([sin_node, -sin_node], axis=1),
    )
    back = lax.all_to_all(back, ("zl", "core", "head"), 0, 0)
    input_grad = run_product(here, back, weights_mine, weights_other)

    dq_sum = (
        dq_own
        + lax.ppermute(dq_others[0], "core", swap).astype(f32)
        + lax.ppermute(dq_others[1], "zl", swap).astype(f32)
        + lax.ppermute(dq_others[2], ("zl", "core"), both_swap).astype(f32)
    )
    return (input_grad, dq_sum.astype(bf16))


def solution(mesh):
    ctx = ("x", "zl", "y", "core")
    split = Mesh(mesh.devices.reshape(4, 2, 4, 2, n_head), ctx + ("head",))
    return jax.shard_map(
        shards,
        mesh=split,
        in_specs=(
            P(ctx, None),
            P(None, "head"),
            P(None, "head"),
            P(ctx, "head"),
            P(ctx, "head"),
            P(ctx),
            P(),
        ),
        out_specs=(P(ctx, "head"), P(ctx, "head")),
        check_vma=False,
    )
```

profile of v0, /device:TPU:1, one launch (start us, length us, event | category | flops | bytes accessed | tf_op | source)
XLA Modules:
  0.0 132.7 jit_solution(7544908292402978712)
XLA Ops:
  0.7 0.9 broadcast_multiply_fusion
  2.3 2.4 %convolution_convert_fusion = bf16[128,128]{1,0:T(8,128)(2,1)S(1)} fusion(bf16[128,8192]{1,0:T(8,128)(2,1)S(1)} %copy-done, bf16[8192,128]{1,0:T(8,128)(2,1)} %param.9), kind=kOutput, calls=%fused_computation | convolution fusion | flops 268451840 | bytes 4227072 | tf_op jit(solution)/shard_map/dot_general | solution.py:440
  4.8 0.7 fusion.15
  6.2 3.3 %collective-permute-start = (bf16[2,2,16,384]{3,2,1,0:T(8,128)(2,1)S(1)}, bf16[2,2,16,384]{3,2,1,0:T(8,128)(2,1)S(1)}, u32[]{:S(2)}, u32[]{:S(2)}) collective-permute-start(bf16[2,2,16,384]{3,2,1,0:T(8,128)(2,1)S(1)} %get-tuple-element.36), channel_id=1, source_target_pairs={{0,4},{4,0},{1,5},{5,1},{2,6},{6,2},{3,7},{7,3},{8,12},{12,8},{9,1... | collective-permute-start | bytes 147464 | tf_op jit(solution)/shard_map/ppermute | solution.py:446
  9.5 0.9 collective-permute-done
  10.5 1.0 select_bitcast_fusion
  11.7 1.7 %collective-permute-done.1 = bf16[2,2,16,384]{3,2,1,0:T(8,128)(2,1)S(1)} collective-permute-done((bf16[2,2,16,384]{3,2,1,0:T(8,128)(2,1)S(1)}, bf16[2,2,16,384]{3,2,1,0:T(8,128)(2,1)S(1)}, u32[]{:S(2)}, u32[]{:S(2)}) %collective-permute-start.1) | collective-permute-done | bytes 49184 | tf_op jit(solution)/shard_map/ppermute | solution.py:449
  13.5 1.4 %broadcast_in_dim.13 = bf16[16,128,384]{2,1,0:T(8,128)(2,1)} broadcast(bf16[128,384]{1,0:T(8,128)(2,1)S(1)} %bitcast.42), dimensions={1,2} | broadcast | bytes 1671168 | tf_op jit(solution)/shard_map/broadcast_in_dim | solution.py:488
  14.8 5.2 %all-to-all-start = ((bf16[16,128,384]{2,1,0:T(8,128)(2,1)}), bf16[16,128,384]{2,1,0:T(8,128)(2,1)}, u32[]{:S(2)}, u32[]{:S(2)}) async-start(bf16[16,128,384]{2,1,0:T(8,128)(2,1)} %broadcast_in_dim.13), calls=%async_computation | async-start | bytes 3145728 | tf_op jit(solution)/shard_map/all_to_all | solution.py:487
  20.6 1.5 %collective-permute-start.3 = (bf16[272,1024]{1,0:T(8,128)(2,1)S(1)}, bf16[272,1024]{1,0:T(8,128)(2,1)S(1)}, u32[]{:S(2)}, u32[]{:S(2)}) collective-permute-start(bf16[272,1024]{1,0:T(8,128)(2,1)S(1)} %concatenate.30.refs_1_), channel_id=1, source_target_pairs={{0,32},{32,0},{1,33},{33,1},{2,34},{34,2},{3,35},{35,3},{4,36},{36... | collective-permute-start | bytes 1671176 | tf_op jit(solution)/shard_map/ppermute | solution.py:478
  22.1 5.2 %collective-permute-start.6 = (bf16[128,128]{1,0:T(8,128)(2,1)S(1)}, bf16[128,128]{1,0:T(8,128)(2,1)S(1)}, u32[]{:S(2)}, u32[]{:S(2)}) collective-permute-start(bf16[128,128]{1,0:T(8,128)(2,1)S(1)} %get-tuple-element.29), channel_id=1, source_target_pairs={{0,3},{1,0},{2,1},{3,2},{4,7},{5,4},{6,5},{7,6},{8,11},{9,8},{10,9... | collective-permute-start | bytes 98312 | tf_op jit(solution)/shard_map/ppermute | solution.py:464
  27.3 1.2 collective-permute-start.5
  28.5 2.1 %collective-permute-start.4 = (bf16[128,128]{1,0:T(8,128)(2,1)S(1)}, bf16[128,128]{1,0:T(8,128)(2,1)S(1)}, u32[]{:S(2)}, u32[]{:S(2)}) collective-permute-start(bf16[128,128]{1,0:T(8,128)(2,1)S(1)} %get-tuple-element.31), channel_id=1, source_target_pairs={{0,1},{1,2},{2,3},{3,0},{4,5},{5,6},{6,7},{7,4},{8,9},{9,10},{10,1... | collective-permute-start | bytes 98312 | tf_op jit(solution)/shard_map/ppermute | solution.py:464
  30.6 2.9 %collective-permute-start.2 = (bf16[272,1024]{1,0:T(8,128)(2,1)S(1)}, bf16[272,1024]{1,0:T(8,128)(2,1)}, u32[]{:S(2)}, u32[]{:S(2)}) collective-permute-start(bf16[272,1024]{1,0:T(8,128)(2,1)S(1)} %concatenate.30.refs_1_), channel_id=1, source_target_pairs={{0,4},{4,0},{1,5},{5,1},{2,6},{6,2},{3,7},{7,3},{8,12},{12,8},{9,1... | collective-permute-start | bytes 1671176 | tf_op jit(solution)/shard_map/ppermute | solution.py:482
  33.5 7.4 %collective-permute-done.5 = bf16[128,128]{1,0:T(8,128)(2,1)S(1)} collective-permute-done((bf16[128,128]{1,0:T(8,128)(2,1)S(1)}, bf16[128,128]{1,0:T(8,128)(2,1)S(1)}, u32[]{:S(2)}, u32[]{:S(2)}) %collective-permute-start.5) | collective-permute-done | bytes 32800 | tf_op jit(solution)/shard_map/ppermute | solution.py:464
  40.9 1.5 %broadcast_in_dim.17 = bf16[16,128,512]{2,1,0:T(8,128)(2,1)} broadcast(bf16[128,512]{1,0:T(8,128)(2,1)S(1)} %pad_maximum_fusion), dimensions={1,2} | broadcast | bytes 2228224 | tf_op jit(solution)/shard_map/broadcast_in_dim | solution.py:468
  42.4 3.0 %collective-permute-start.7 = (bf16[272,1024]{1,0:T(8,128)(2,1)S(1)}, bf16[272,1024]{1,0:T(8,128)(2,1)}, u32[]{:S(2)}, u32[]{:S(2)}) collective-permute-start(bf16[272,1024]{1,0:T(8,128)(2,1)S(1)} %collective-permute-done.3.refs_3_), channel_id=1, source_target_pairs={{0,4},{4,0},{1,5},{5,1},{2,6},{6,2},{3,7},{7,3},{8,12},{12,8},{9,1... | collective-permute-start | bytes 1671176 | tf_op jit(solution)/shard_map/ppermute | solution.py:484
  45.5 6.7 %all-to-all-start.1 = ((bf16[16,128,512]{2,1,0:T(8,128)(2,1)}), bf16[16,128,512]{2,1,0:T(8,128)(2,1)}, u32[]{:S(2)}, u32[]{:S(2)}) async-start(bf16[16,128,512]{2,1,0:T(8,128)(2,1)} %broadcast_in_dim.17), calls=%async_computation.1 | async-start | bytes 4194304 | tf_op jit(solution)/shard_map/all_to_all | solution.py:490
  52.2 9.3 %shard_map.86.refs_5_ = f32[16,512]{1,0:T(8,128)S(1)} custom-call(s32[4]{0:T(128)S(1)} %pad_add_fusion.1.place_ref, s32[128]{0:T(128)S(1)} %copy-done.2, bf16[2048,384]{1,0:T(8,128)(2,1)} %bitcast.18.refs_0_, bf16[272,1024]{1,0:T(8,128)(2,1)S(1)} %concatenate.30.refs_1_, bf16[272,1024]{1,0:T(8,128)(2,1)} %collective-permute-done.2.refs_2_, ...), custom_call_target="tpu_custom_call" | custom-call | flops 8589934592 | bytes 4194304 | tf_op jit(solution)/shard_map/pallas_call | solution.py:285
  61.5 1.3 collective-permute-start.10
  63.7 1.6 %collective-permute-done.10.refs_8_ = f32[16,512]{1,0:T(8,128)S(1)} collective-permute-done((f32[16,512]{1,0:T(8,128)S(1)}, f32[16,512]{1,0:T(8,128)S(1)}, u32[]{:S(2)}, u32[]{:S(2)}) %collective-permute-start.10) | collective-permute-done | bytes 32800 | tf_op jit(solution)/shard_map/ppermute | solution.py:499
  67.2 14.4 %shard_map.87 = (bf16[2048,256]{1,0:T(8,128)(2,1)}, f32[128,1024]{1,0:T(8,128)}, bf16[128,1024]{1,0:T(8,128)(2,1)}, bf16[128,1024]{1,0:T(8,128)(2,1)}, bf16[128,1024]{1,0:T(8,128)(2,1)}) custom-call(s32[4]{0:T(128)} %copy-done.3, s32[128]{0:T(128)} %order_ref.3, bf16[2048,384]{1,0:T(8,128)(2,1)} %bitcast.18.refs_0_, bf16[272,1024]{1,0:T(8,128)(2,1)} %copy-done.1, ...), custom_call_target="tpu_custom_call" | custom-call | flops 17179869184 | bytes 8388608 | tf_op jit(solution)/shard_map/pallas_call | solution.py:306
  81.6 1.5 %collective-permute-start.11 = (bf16[2048,512]{1,0:T(8,128)(2,1)}, bf16[2048,512]{1,0:T(8,128)(2,1)}, u32[]{:S(2)}, u32[]{:S(2)}) collective-permute-start(bf16[2048,512]{1,0:T(8,128)(2,1)} %bitcast.24.mine_ref), channel_id=1, source_target_pairs={{0,4},{4,0},{1,5},{5,1},{2,6},{6,2},{3,7},{7,3},{8,12},{12,8},{9,1... | collective-permute-start | bytes 6291464 | tf_op jit(solution)/shard_map/ppermute | solution.py:506
  83.1 8.6 %all-to-all-start.2 = ((bf16[16,128,256]{2,1,0:T(8,128)(2,1)}), bf16[16,128,256]{2,1,0:T(8,128)(2,1)S(1)}, u32[]{:S(2)}, u32[]{:S(2)}) async-start(bf16[16,128,256]{2,1,0:T(8,128)(2,1)} %bitcast.40), calls=%async_computation.2 | async-start | bytes 2097152 | tf_op jit(solution)/shard_map/all_to_all | solution.py:508
  92.3 0.7 collective-permute-start.13
  93.0 1.1 collective-permute-start.14
  94.2 14.5 %all-to-all-done.2.parts_ref = bf16[16,128,256]{2,1,0:T(8,128)(2,1)S(1)} async-done(((bf16[16,128,256]{2,1,0:T(8,128)(2,1)}), bf16[16,128,256]{2,1,0:T(8,128)(2,1)S(1)}, u32[]{:S(2)}, u32[]{:S(2)}) %all-to-all-start.2) | async-done | bytes 1048608 | tf_op jit(solution)/shard_map/all_to_all | solution.py:508
  108.7 1.4 %shard_map.88 = bf16[16,32,256]{2,1,0:T(8,128)(2,1)} custom-call(s32[3]{0:T(128)S(1)} %pad_add_fusion.place_ref, bf16[16,128,256]{2,1,0:T(8,128)(2,1)S(1)} %all-to-all-done.2.parts_ref, f32[128,128]{1,0:T(8,128)S(1)} %get-tuple-element.48.cos_ref, f32[128,128]{1,0:T(8,128)S(1)} %get-tuple-element.49.sin_ref), custom_call_target="tpu_custom_call" | custom-call | flops 655360 | bytes 2097152 | tf_op jit(solution)/shard_map/pallas_call | solution.py:355
  110.1 6.5 %all-to-all-start.3 = ((bf16[16,32,256]{2,1,0:T(8,128)(2,1)}), bf16[16,32,256]{2,1,0:T(8,128)(2,1)S(1)}, u32[]{:S(2)}, u32[]{:S(2)}) async-start(bf16[16,32,256]{2,1,0:T(8,128)(2,1)} %shard_map.88), calls=%async_computation.3 | async-start | bytes 524288 | tf_op jit(solution)/shard_map/all_to_all | solution.py:528
  116.6 2.1 %add_convert_fusion = bf16[128,1024]{1,0:T(8,128)(2,1)} fusion(bf16[128,1024]{1,0:T(8,128)(2,1)} %collective-permute-done.14, bf16[128,1024]{1,0:T(8,128)(2,1)} %collective-permute-done.13, f32[128,1024]{1,0:T(8,128)} %get-tuple-element.20, bf16[128,1024]{1,0:T(8,128)(2,1)S(1)} %collective-permute-done.12), kind=kLoop, calls=%fused_computation.1 | loop fusion | flops 917504 | bytes 1572864 | tf_op jit(solution)/shard_map/convert_element_type | solution.py:537
  118.6 9.5 %all-to-all-done.3.back_ref = bf16[16,32,256]{2,1,0:T(8,128)(2,1)S(1)} async-done(((bf16[16,32,256]{2,1,0:T(8,128)(2,1)}), bf16[16,32,256]{2,1,0:T(8,128)(2,1)S(1)}, u32[]{:S(2)}, u32[]{:S(2)}) %all-to-all-start.3) | async-done | bytes 262176 | tf_op jit(solution)/shard_map/all_to_all | solution.py:528
  128.2 4.5 %shard_map.89 = bf16[128,2048]{1,0:T(8,128)(2,1)} custom-call(s32[3]{0:T(128)S(1)} %pad_add_fusion.place_ref, bf16[16,32,256]{2,1,0:T(8,128)(2,1)S(1)} %all-to-all-done.3.back_ref, bf16[2048,512]{1,0:T(8,128)(2,1)} %bitcast.24.mine_ref, bf16[2048,512]{1,0:T(8,128)(2,1)} %collective-permute-done.11.other_ref), custom_call_target="tpu_custom_call" | custom-call | flops 536870912 | bytes 5242880 | tf_op jit(solution)/shard_map/pallas_call | solution.py:396
  (67 shorter events, 5.6 us)
Async XLA Ops:
  0.6 1.7 %copy-start = (bf16[128,8192]{1,0:T(8,128)(2,1)S(1)}, bf16[128,8192]{1,0:T(8,128)(2,1)}, u32[]{:S(2)}) copy-start(bf16[128,8192]{1,0:T(8,128)(2,1)} %param.7) | copy-start | bytes 6291460
  2.3 2.4 %copy-start.6 = (bf16[8192,128]{1,0:T(8,128)(2,1)S(1)}, bf16[8192,128]{1,0:T(8,128)(2,1)}, u32[]{:S(2)}) copy-start(bf16[8192,128]{1,0:T(8,128)(2,1)} %param.8) | copy-start | bytes 6291460
  4.7 6.8 %copy-start.12 = (s32[128]{0:T(128)S(1)}, s32[128]{0:T(128)}, u32[]{:S(2)}) copy-start(s32[128]{0:T(128)} %param.12) | copy-start | bytes 1540
  6.2 4.2 %collective-permute-start = (bf16[2,2,16,384]{3,2,1,0:T(8,128)(2,1)S(1)}, bf16[2,2,16,384]{3,2,1,0:T(8,128)(2,1)S(1)}, u32[]{:S(2)}, u32[]{:S(2)}) collective-permute-start(bf16[2,2,16,384]{3,2,1,0:T(8,128)(2,1)S(1)} %get-tuple-element.36), channel_id=1, source_target_pairs={{0,4},{4,0},{1,5},{5,1},{2,6},{6,2},{3,7},{7,3},{8,12},{12,8},{9,1... | collective-permute-start | bytes 147464 | tf_op jit(solution)/shard_map/ppermute | solution.py:446
  10.4 3.0 %collective-permute-start.1 = (bf16[2,2,16,384]{3,2,1,0:T(8,128)(2,1)S(1)}, bf16[2,2,16,384]{3,2,1,0:T(8,128)(2,1)S(1)}, u32[]{:S(2)}, u32[]{:S(2)}) collective-permute-start(bf16[2,2,16,384]{3,2,1,0:T(8,128)(2,1)S(1)} %get-tuple-element.35), channel_id=1, source_target_pairs={{0,32},{32,0},{1,33},{33,1},{2,34},{34,2},{3,35},{35,3},{4,36},{36... | collective-permute-start | bytes 147464 | tf_op jit(solution)/shard_map/ppermute | solution.py:449
  13.4 6.7 %copy-start.7 = (bf16[128,1024]{1,0:T(8,128)(2,1)S(1)}, bf16[128,1024]{1,0:T(8,128)(2,1)}, u32[]{:S(2)}) copy-start(bf16[128,1024]{1,0:T(8,128)(2,1)} %param.10) | copy-start | bytes 786436
  13.5 6.7 %copy-start.8 = (bf16[128,1024]{1,0:T(8,128)(2,1)S(1)}, bf16[128,1024]{1,0:T(8,128)(2,1)}, u32[]{:S(2)}) copy-start(bf16[128,1024]{1,0:T(8,128)(2,1)} %param.11) | copy-start | bytes 786436
  14.8 30.6 %all-to-all-start = ((bf16[16,128,384]{2,1,0:T(8,128)(2,1)}), bf16[16,128,384]{2,1,0:T(8,128)(2,1)}, u32[]{:S(2)}, u32[]{:S(2)}) async-start(bf16[16,128,384]{2,1,0:T(8,128)(2,1)} %broadcast_in_dim.13), calls=%async_computation | async-start | bytes 3145728 | tf_op jit(solution)/shard_map/all_to_all | solution.py:487
  20.6 31.6 %copy-start.1 = (bf16[272,1024]{1,0:T(8,128)(2,1)}, bf16[272,1024]{1,0:T(8,128)(2,1)S(1)}, u32[]{:S(2)}) copy-start(bf16[272,1024]{1,0:T(8,128)(2,1)S(1)} %concatenate.30.refs_1_) | copy-start | bytes 1671172
  20.6 20.3 %collective-permute-start.3 = (bf16[272,1024]{1,0:T(8,128)(2,1)S(1)}, bf16[272,1024]{1,0:T(8,128)(2,1)S(1)}, u32[]{:S(2)}, u32[]{:S(2)}) collective-permute-start(bf16[272,1024]{1,0:T(8,128)(2,1)S(1)} %concatenate.30.refs_1_), channel_id=1, source_target_pairs={{0,32},{32,0},{1,33},{33,1},{2,34},{34,2},{3,35},{35,3},{4,36},{36... | collective-permute-start | bytes 1671176 | tf_op jit(solution)/shard_map/ppermute | solution.py:478
  22.1 11.4 %collective-permute-start.6 = (bf16[128,128]{1,0:T(8,128)(2,1)S(1)}, bf16[128,128]{1,0:T(8,128)(2,1)S(1)}, u32[]{:S(2)}, u32[]{:S(2)}) collective-permute-start(bf16[128,128]{1,0:T(8,128)(2,1)S(1)} %get-tuple-element.29), channel_id=1, source_target_pairs={{0,3},{1,0},{2,1},{3,2},{4,7},{5,4},{6,5},{7,6},{8,11},{9,8},{10,9... | collective-permute-start | bytes 98312 | tf_op jit(solution)/shard_map/ppermute | solution.py:464
  27.3 13.5 %collective-permute-start.5 = (bf16[128,128]{1,0:T(8,128)(2,1)S(1)}, bf16[128,128]{1,0:T(8,128)(2,1)S(1)}, u32[]{:S(2)}, u32[]{:S(2)}) collective-permute-start(bf16[128,128]{1,0:T(8,128)(2,1)S(1)} %get-tuple-element.30), channel_id=1, source_target_pairs={{0,2},{1,3},{2,0},{3,1},{4,6},{5,7},{6,4},{7,5},{8,10},{9,11},{10,... | collective-permute-start | bytes 98312 | tf_op jit(solution)/shard_map/ppermute | solution.py:464
  28.5 12.4 %collective-permute-start.4 = (bf16[128,128]{1,0:T(8,128)(2,1)S(1)}, bf16[128,128]{1,0:T(8,128)(2,1)S(1)}, u32[]{:S(2)}, u32[]{:S(2)}) collective-permute-start(bf16[128,128]{1,0:T(8,128)(2,1)S(1)} %get-tuple-element.31), channel_id=1, source_target_pairs={{0,1},{1,2},{2,3},{3,0},{4,5},{5,6},{6,7},{7,4},{8,9},{9,10},{10,1... | collective-permute-start | bytes 98312 | tf_op jit(solution)/shard_map/ppermute | solution.py:464
  30.6 21.6 %collective-permute-start.2 = (bf16[272,1024]{1,0:T(8,128)(2,1)S(1)}, bf16[272,1024]{1,0:T(8,128)(2,1)}, u32[]{:S(2)}, u32[]{:S(2)}) collective-permute-start(bf16[272,1024]{1,0:T(8,128)(2,1)S(1)} %concatenate.30.refs_1_), channel_id=1, source_target_pairs={{0,4},{4,0},{1,5},{5,1},{2,6},{6,2},{3,7},{7,3},{8,12},{12,8},{9,1... | collective-permute-start | bytes 1671176 | tf_op jit(solution)/shard_map/ppermute | solution.py:482
  40.9 11.3 %copy-start.4 = (bf16[272,1024]{1,0:T(8,128)(2,1)}, bf16[272,1024]{1,0:T(8,128)(2,1)S(1)}, u32[]{:S(2)}) copy-start(bf16[272,1024]{1,0:T(8,128)(2,1)S(1)} %collective-permute-done.3.refs_3_) | copy-start | bytes 1671172
  42.4 9.7 %collective-permute-start.7 = (bf16[272,1024]{1,0:T(8,128)(2,1)S(1)}, bf16[272,1024]{1,0:T(8,128)(2,1)}, u32[]{:S(2)}, u32[]{:S(2)}) collective-permute-start(bf16[272,1024]{1,0:T(8,128)(2,1)S(1)} %collective-permute-done.3.refs_3_), channel_id=1, source_target_pairs={{0,4},{4,0},{1,5},{5,1},{2,6},{6,2},{3,7},{7,3},{8,12},{12,8},{9,1... | collective-permute-start | bytes 1671176 | tf_op jit(solution)/shard_map/ppermute | solution.py:484
  45.5 6.7 %copy-start.3 = (s32[4]{0:T(128)}, s32[4]{0:T(128)S(1)}, u32[]{:S(2)}) copy-start(s32[4]{0:T(128)S(1)} %pad_add_fusion.1.place_ref) | copy-start | bytes 52
  45.5 6.7 %copy-start.2 = (s32[128]{0:T(128)S(1)}, s32[128]{0:T(128)}, u32[]{:S(2)}) copy-start(s32[128]{0:T(128)} %order_ref.3) | copy-start | bytes 1540
  45.5 36.1 %all-to-all-start.1 = ((bf16[16,128,512]{2,1,0:T(8,128)(2,1)}), bf16[16,128,512]{2,1,0:T(8,128)(2,1)}, u32[]{:S(2)}, u32[]{:S(2)}) async-start(bf16[16,128,512]{2,1,0:T(8,128)(2,1)} %broadcast_in_dim.17), calls=%async_computation.1 | async-start | bytes 4194304 | tf_op jit(solution)/shard_map/all_to_all | solution.py:490
  61.5 4.5 %copy-start.5 = (f32[16,512]{1,0:T(8,128)}, f32[16,512]{1,0:T(8,128)S(1)}, u32[]{:S(2)}) copy-start(f32[16,512]{1,0:T(8,128)S(1)} %shard_map.86.refs_5_) | copy-start | bytes 98308
  61.5 3.8 %collective-permute-start.10 = (f32[16,512]{1,0:T(8,128)S(1)}, f32[16,512]{1,0:T(8,128)S(1)}, u32[]{:S(2)}, u32[]{:S(2)}) collective-permute-start(f32[16,512]{1,0:T(8,128)S(1)} %shard_map.86.refs_5_), channel_id=1, source_target_pairs={{0,36},{4,32},{32,4},{36,0},{1,37},{5,33},{33,5},{37,1},{2,38},{6,... | collective-permute-start | bytes 98312 | tf_op jit(solution)/shard_map/ppermute | solution.py:499
  62.8 3.2 %collective-permute-start.9 = (f32[16,512]{1,0:T(8,128)S(1)}, f32[16,512]{1,0:T(8,128)S(1)}, u32[]{:S(2)}, u32[]{:S(2)}) collective-permute-start(f32[16,512]{1,0:T(8,128)S(1)} %shard_map.86.refs_5_), channel_id=1, source_target_pairs={{0,32},{32,0},{1,33},{33,1},{2,34},{34,2},{3,35},{35,3},{4,36},{36... | collective-permute-start | bytes 98312 | tf_op jit(solution)/shard_map/ppermute | solution.py:498
  63.2 2.8 %collective-permute-start.8 = (f32[16,512]{1,0:T(8,128)S(1)}, f32[16,512]{1,0:T(8,128)S(1)}, u32[]{:S(2)}, u32[]{:S(2)}) collective-permute-start(f32[16,512]{1,0:T(8,128)S(1)} %shard_map.86.refs_5_), channel_id=1, source_target_pairs={{0,4},{4,0},{1,5},{5,1},{2,6},{6,2},{3,7},{7,3},{8,12},{12,8},{9,1... | collective-permute-start | bytes 98312 | tf_op jit(solution)/shard_map/ppermute | solution.py:497
  65.3 0.7 copy-start.9
  66.0 0.6 copy-start.10
  66.6 0.6 copy-start.11
  81.6 46.6 %collective-permute-start.11 = (bf16[2048,512]{1,0:T(8,128)(2,1)}, bf16[2048,512]{1,0:T(8,128)(2,1)}, u32[]{:S(2)}, u32[]{:S(2)}) collective-permute-start(bf16[2048,512]{1,0:T(8,128)(2,1)} %bitcast.24.mine_ref), channel_id=1, source_target_pairs={{0,4},{4,0},{1,5},{5,1},{2,6},{6,2},{3,7},{7,3},{8,12},{12,8},{9,1... | collective-permute-start | bytes 6291464 | tf_op jit(solution)/shard_map/ppermute | solution.py:506
  83.1 25.6 %all-to-all-start.2 = ((bf16[16,128,256]{2,1,0:T(8,128)(2,1)}), bf16[16,128,256]{2,1,0:T(8,128)(2,1)S(1)}, u32[]{:S(2)}, u32[]{:S(2)}) async-start(bf16[16,128,256]{2,1,0:T(8,128)(2,1)} %bitcast.40), calls=%async_computation.2 | async-start | bytes 2097152 | tf_op jit(solution)/shard_map/all_to_all | solution.py:508
  91.9 24.7 %collective-permute-start.12 = (bf16[128,1024]{1,0:T(8,128)(2,1)}, bf16[128,1024]{1,0:T(8,128)(2,1)S(1)}, u32[]{:S(2)}, u32[]{:S(2)}) collective-permute-start(bf16[128,1024]{1,0:T(8,128)(2,1)} %get-tuple-element.21), channel_id=1, source_target_pairs={{0,4},{4,0},{1,5},{5,1},{2,6},{6,2},{3,7},{7,3},{8,12},{12,8},{9,1... | collective-permute-start | bytes 786440 | tf_op jit(solution)/shard_map/ppermute | solution.py:533
  92.3 24.3 %collective-permute-start.13 = (bf16[128,1024]{1,0:T(8,128)(2,1)}, bf16[128,1024]{1,0:T(8,128)(2,1)}, u32[]{:S(2)}, u32[]{:S(2)}) collective-permute-start(bf16[128,1024]{1,0:T(8,128)(2,1)} %get-tuple-element.22), channel_id=1, source_target_pairs={{0,32},{32,0},{1,33},{33,1},{2,34},{34,2},{3,35},{35,3},{4,36},{36... | collective-permute-start | bytes 786440 | tf_op jit(solution)/shard_map/ppermute | solution.py:534
  93.0 23.6 %collective-permute-start.14 = (bf16[128,1024]{1,0:T(8,128)(2,1)}, bf16[128,1024]{1,0:T(8,128)(2,1)}, u32[]{:S(2)}, u32[]{:S(2)}) collective-permute-start(bf16[128,1024]{1,0:T(8,128)(2,1)} %get-tuple-element.23), channel_id=1, source_target_pairs={{0,36},{4,32},{32,4},{36,0},{1,37},{5,33},{33,5},{37,1},{2,38},{6,... | collective-permute-start | bytes 786440 | tf_op jit(solution)/shard_map/ppermute | solution.py:535
  110.1 18.1 %all-to-all-start.3 = ((bf16[16,32,256]{2,1,0:T(8,128)(2,1)}), bf16[16,32,256]{2,1,0:T(8,128)(2,1)S(1)}, u32[]{:S(2)}, u32[]{:S(2)}) async-start(bf16[16,32,256]{2,1,0:T(8,128)(2,1)} %shard_map.88), calls=%async_computation.3 | async-start | bytes 524288 | tf_op jit(solution)/shard_map/all_to_all | solution.py:528
where the time goes:
time: 132 us; the launch traced here: 133 us
  starting transfers between devices  52.2 us (40%)
  waiting for transfers between devices  36.3 us (27%)
  Pallas kernels  29.6 us (22%)
  other arithmetic  5.21 us (4%)
  local copies, waits for them, and re-layouts  5.17 us (4%)
  matrix products  3.13 us (2%)
    all_to_all x1, waiting for transfers between devices, shards(): lax.all_to_all(grads.reshape(16, row_count, 2 * head_dim), ('x', 'y'), 0, 0)  14.5 us
    pallas_call x1, Pallas kernels, run_grads(): pl.pallas_call(functools.partial(grads_kernel, factor=scaling * log2e, sc...  14.4 us
    all_to_all x1, waiting for transfers between devices, shards(): back = lax.all_to_all(back, ('zl', 'core', 'head'), 0, 0)  9.52 us
    pallas_call x1, Pallas kernels, run_stats(): pl.pallas_call(functools.partial(stats_kernel, factor=scaling * log2e), o...  9.26 us
    all_to_all x1, starting transfers between devices, shards(): lax.all_to_all(grads.reshape(16, row_count, 2 * head_dim), ('x', 'y'), 0, 0)  8.64 us
    ppermute x3, starting transfers between devices, shards(): lax.ppermute(pick(weight_shares, (head + s) % n_head, 0), 'head', head_pe...  8.45 us
    ppermute x3, waiting for transfers between devices, shards(): lax.ppermute(pick(weight_shares, (head + s) % n_head, 0), 'head', head_pe...  7.38 us
    all_to_all x1, starting transfers between devices, shards(): weights_mine = lax.all_to_all(weight_rows, ('x', 'y'), 0, 0)  6.67 us
  transfers between devices with their start and end apart: 19, of which 7 were waited for; matrix products, arithmetic and copies ran while one was open for 4% of the time, Pallas kernels for 19%

commit v1 on v0

--- a/solution.py
+++ b/solution.py
@@ -325,7 +325,7 @@
         + [pltpu.SemaphoreType.DMA((5,))],
         compiler_params=pltpu.CompilerParams(vmem_limit_bytes=57 * 1024 * 1024),
         cost_estimate=pl.CostEstimate(
-            flops=16 * rows * tokens * head_dim,
+            flops=4 * rows * tokens * head_dim,
             bytes_accessed=8 * 1024 * 1024,
             transcendentals=rows * tokens // 2,
         ),
@@ -364,31 +364,37 @@
     )(place, parts, cos_wide, sin_wide)
 
 
-def product_kernel(place_ref, back_ref, mine_ref, other_ref, out_ref, left_mine, left_other):
-    head_dim = back_ref.shape[2] // 2
+def product_kernel(place_ref, back_ref, own_ref, mine_ref, other_ref, out_ref, *left):
+    left_own, left_mine, left_other = left
+    width = back_ref.shape[2]
+    head_dim = width // 2
     first = pl.multiple_of(place_ref[1] * head_dim, head_dim)
     second = pl.multiple_of(head_dim - first, head_dim)
-    for source in range(back_ref.shape[0]):
-        quarter, shift = source // n_head, source % n_head
-        sender = quarter * n_head + (place_ref[2] + n_head - shift) % n_head
-        cols = pl.ds(shift * head_dim, head_dim)
-        for block in range(2):
-            to = pl.ds(block * block_len + quarter * granule, granule)
-            at = pl.ds(block * granule, granule)
-            left_mine[to, cols] = back_ref[sender, at, pl.ds(first, head_dim)]
-            left_other[to, cols] = back_ref[sender, at, pl.ds(second, head_dim)]
+    for shift in range(n_head):
+        for quarter in range(4):
+            sender = quarter * n_head + (place_ref[2] + n_head - shift) % n_head
+            for block in range(2):
+                to = pl.ds(block * block_len + quarter * granule, granule)
+                at = pl.ds(block * granule, granule)
+                if shift == 0:
+                    left_own[to, :] = back_ref[sender, at, :]
+                else:
+                    cols = pl.ds((shift - 1) * head_dim, head_dim)
+                    left_mine[to, cols] = back_ref[sender, at, pl.ds(first, head_dim)]
+                    left_other[to, cols] = back_ref[sender, at, pl.ds(second, head_dim)]
+
+    def times(left, right):
+        return lax.dot_general(left[...], right, contract_last, preferred_element_type=jnp.float32)
+
     for tile in range(out_ref.shape[1] // 512):
         at = pl.ds(tile * 512, 512)
-        total = lax.dot_general(
-            left_mine[...], mine_ref[at, :], contract_last, preferred_element_type=jnp.float32
-        )
-        total += lax.dot_general(
-            left_other[...], other_ref[at, :], contract_last, preferred_element_type=jnp.float32
-        )
+        total = times(left_own, own_ref[at, :])
+        total += times(left_mine, mine_ref[at, :])
+        total += times(left_other, other_ref[at, :])
         out_ref[:, at] = total.astype(jnp.bfloat16)
 
 
-def run_product(place, back, mine, other):
+def run_product(place, back, own, mine, other):
     smem = pl.BlockSpec(memory_space=pltpu.SMEM)
     vmem = pl.BlockSpec(memory_space=pltpu.VMEM)
     row_count = back.shape[0] * back.shape[1] // n_head
@@ -396,16 +402,17 @@
     return pl.pallas_call(
         product_kernel,
         out_shape=jax.ShapeDtypeStruct((row_count, out_width), jnp.bfloat16),
-        in_specs=[smem] + [vmem] * 3,
+        in_specs=[smem] + [vmem] * 4,
         out_specs=vmem,
-        scratch_shapes=[pltpu.VMEM((row_count, depth), jnp.bfloat16)] * 2,
+        scratch_shapes=[pltpu.VMEM((row_count, back.shape[2]), jnp.bfloat16)]
+        + [pltpu.VMEM((row_count, depth), jnp.bfloat16)] * 2,
         compiler_params=pltpu.CompilerParams(vmem_limit_bytes=24 * 1024 * 1024),
         cost_estimate=pl.CostEstimate(
             flops=4 * row_count * depth * out_width,
             bytes_accessed=5 * 1024 * 1024,
             transcendentals=0,
         ),
-    )(place, back, mine, other)
+    )(place, back, own, mine, other)
 
 
 def shards(layer_input, key_weight, value_weight, queries, out_grad, doc_start, block_order):
@@ -460,12 +467,12 @@
         core_is_one, weight_share(value_weight), weight_share(key_weight)
     )
     node, weight_shares = lax.optimization_barrier((node, weight_shares))
-    weight_rows = [pick(weight_shares, head, 0)] + [
+    weight_rows = [
         lax.ppermute(pick(weight_shares, (head + s) % n_head, 0), "head", head_perm(s))
         for s in (1, 2, 3)
     ]
     weight_rows = jnp.concatenate(weight_rows, axis=1)[None]
-    weight_rows = jnp.broadcast_to(weight_rows, (16, share, n_head * head_dim))
+    weight_rows = jnp.broadcast_to(weight_rows, (16, share, (n_head - 1) * head_dim))
 
     def per_column(v):
         return jnp.broadcast_to(v.reshape(2, 1, block_len), (2, groups, block_len)).reshape(1, rows)
@@ -502,9 +509,13 @@
         place, block_order, gathered, packs, stats_all, scaling, tokens, head_dim, rows
     )
     grads, weights_mine = lax.optimization_barrier((grads, weights_mine))
-    weights_mine = weights_mine.reshape(out_width, n_head * head_dim)
+    weights_mine = weights_mine.reshape(out_width, (n_head - 1) * head_dim)
     weights_other = lax.ppermute(weights_mine, "core", swap)
 
+    weights_own = jnp.concatenate(
+        [lax.dynamic_slice_in_dim(w, head * out_width, out_width) for w in (key_weight, value_weight)],
+        axis=1,
+    )
     grads = lax.all_to_all(
         grads.reshape(16, row_count, 2 * head_dim), ("x", "y"), 0, 0
     )
@@ -526,7 +537,7 @@
         jnp.concatenate([sin_node, -sin_node], axis=1),
     )
     back = lax.all_to_all(back, ("zl", "core", "head"), 0, 0)
-    input_grad = run_product(here, back, weights_mine, weights_other)
+    input_grad = run_product(here, back, weights_own, weights_mine, weights_other)
 
     dq_sum = (
         dq_own

time: 132 us -> 131 us (level)
  waiting for transfers between devices: 36.3 us -> 32.2 us
  local copies, waits for them, and re-layouts: 5.17 us -> 6.83 us
    all_to_all x1, waiting for transfers between devices: 14.5 us -> 10.6 us  [shards(): lax.all_to_all(grads.reshape(16, row_count, 2 * head_dim), ('x', 'y'), 0, 0)]
    dynamic_slice x0 -> x1, local copies, waits for them, and re-layouts: none -> 2.26 us  [shards(): lax.dynamic_slice_in_dim(w, head * out_width, out_width)]
    all_to_all x1, starting transfers between devices: 6.45 us -> 8.47 us  [shards(): back = lax.all_to_all(back, ('zl', 'core', 'head'), 0, 0)]
    concatenate x0 -> x1, other arithmetic: none -> 1.37 us  [shards(): jnp.concatenate([lax.dynamic_slice_in_dim(w, head * out_width, out_width)...]
  transfers between devices with their start and end apart: 19 -> 19, of which waited for: 7 -> 7; matrix products, arithmetic and copies ran while one was open for 4% -> 7% of each run, Pallas kernels for 19% -> 19%
where the time goes in v1:
time: 131 us; the launch traced here: 132 us
  starting transfers between devices  52.8 us (40%)
  waiting for transfers between devices  32.2 us (25%)
  Pallas kernels  29.3 us (22%)
  local copies, waits for them, and re-layouts  6.83 us (5%)
  other arithmetic  6.49 us (5%)
  matrix products  3.13 us (2%)
    pallas_call x1, Pallas kernels, run_grads(): pl.pallas_call(functools.partial(grads_kernel, factor=scaling * log2e, sc...  14.5 us
    all_to_all x1, waiting for transfers between devices, shards(): lax.all_to_all(grads.reshape(16, row_count, 2 * head_dim), ('x', 'y'), 0, 0)  10.6 us
    pallas_call x1, Pallas kernels, run_stats(): pl.pallas_call(functools.partial(stats_kernel, factor=scaling * log2e), o...  9.3 us
    all_to_all x1, starting transfers between devices, shards(): lax.all_to_all(grads.reshape(16, row_count, 2 * head_dim), ('x', 'y'), 0, 0)  8.58 us
    all_to_all x1, starting transfers between devices, shards(): back = lax.all_to_all(back, ('zl', 'core', 'head'), 0, 0)  8.47 us
    ppermute x3, starting transfers between devices, shards(): lax.ppermute(pick(weight_shares, (head + s) % n_head, 0), 'head', head_pe...  8.45 us
    all_to_all x1, waiting for transfers between devices, shards(): back = lax.all_to_all(back, ('zl', 'core', 'head'), 0, 0)  8.22 us
    ppermute x3, waiting for transfers between devices, shards(): lax.ppermute(pick(weight_shares, (head + s) % n_head, 0), 'head', head_pe...  7.39 us
  transfers between devices with their start and end apart: 19, of which 7 were waited for; matrix products, arithmetic and copies ran while one was open for 7% of the time, Pallas kernels for 19%

profile of v1, /device:TPU:1, one launch (start us, length us, event | category | flops | bytes accessed | tf_op | source)
XLA Modules:
  0.0 131.8 jit_solution(4493079677426745912)
XLA Ops:
  0.7 0.9 broadcast_multiply_fusion
  2.3 2.4 %convolution_convert_fusion = bf16[128,128]{1,0:T(8,128)(2,1)S(1)} fusion(bf16[128,8192]{1,0:T(8,128)(2,1)S(1)} %copy-done, bf16[8192,128]{1,0:T(8,128)(2,1)} %param.9), kind=kOutput, calls=%fused_computation | convolution fusion | flops 268451840 | bytes 4227072 | tf_op jit(solution)/shard_map/dot_general | solution.py:447
  6.3 3.3 %collective-permute-start = (bf16[2,2,16,384]{3,2,1,0:T(8,128)(2,1)S(1)}, bf16[2,2,16,384]{3,2,1,0:T(8,128)(2,1)S(1)}, u32[]{:S(2)}, u32[]{:S(2)}) collective-permute-start(bf16[2,2,16,384]{3,2,1,0:T(8,128)(2,1)S(1)} %get-tuple-element.35), channel_id=1, source_target_pairs={{0,4},{4,0},{1,5},{5,1},{2,6},{6,2},{3,7},{7,3},{8,12},{12,8},{9,1... | collective-permute-start | bytes 147464 | tf_op jit(solution)/shard_map/ppermute | solution.py:453
  9.6 0.9 collective-permute-done
  10.6 1.0 select_bitcast_fusion
  11.6 1.9 %collective-permute-done.1 = bf16[2,2,16,384]{3,2,1,0:T(8,128)(2,1)S(1)} collective-permute-done((bf16[2,2,16,384]{3,2,1,0:T(8,128)(2,1)S(1)}, bf16[2,2,16,384]{3,2,1,0:T(8,128)(2,1)S(1)}, u32[]{:S(2)}, u32[]{:S(2)}) %collective-permute-start.1) | collective-permute-done | bytes 49184 | tf_op jit(solution)/shard_map/ppermute | solution.py:456
  13.6 1.4 %broadcast_in_dim.13 = bf16[16,128,384]{2,1,0:T(8,128)(2,1)} broadcast(bf16[128,384]{1,0:T(8,128)(2,1)S(1)} %bitcast.40), dimensions={1,2} | broadcast | bytes 1671168 | tf_op jit(solution)/shard_map/broadcast_in_dim | solution.py:495
  15.0 5.2 %all-to-all-start = ((bf16[16,128,384]{2,1,0:T(8,128)(2,1)}), bf16[16,128,384]{2,1,0:T(8,128)(2,1)}, u32[]{:S(2)}, u32[]{:S(2)}) async-start(bf16[16,128,384]{2,1,0:T(8,128)(2,1)} %broadcast_in_dim.13), calls=%async_computation | async-start | bytes 3145728 | tf_op jit(solution)/shard_map/all_to_all | solution.py:494
  20.9 1.5 %collective-permute-start.3 = (bf16[272,1024]{1,0:T(8,128)(2,1)S(1)}, bf16[272,1024]{1,0:T(8,128)(2,1)S(1)}, u32[]{:S(2)}, u32[]{:S(2)}) collective-permute-start(bf16[272,1024]{1,0:T(8,128)(2,1)S(1)} %concatenate.33.refs_1_), channel_id=1, source_target_pairs={{0,32},{32,0},{1,33},{33,1},{2,34},{34,2},{3,35},{35,3},{4,36},{36... | collective-permute-start | bytes 1671176 | tf_op jit(solution)/shard_map/ppermute | solution.py:485
  22.5 5.2 %collective-permute-start.6 = (bf16[128,128]{1,0:T(8,128)(2,1)S(1)}, bf16[128,128]{1,0:T(8,128)(2,1)S(1)}, u32[]{:S(2)}, u32[]{:S(2)}) collective-permute-start(bf16[128,128]{1,0:T(8,128)(2,1)S(1)} %get-tuple-element.29), channel_id=1, source_target_pairs={{0,3},{1,0},{2,1},{3,2},{4,7},{5,4},{6,5},{7,6},{8,11},{9,8},{10,9... | collective-permute-start | bytes 98312 | tf_op jit(solution)/shard_map/ppermute | solution.py:471
  27.7 1.2 collective-permute-start.5
  28.8 2.1 %collective-permute-start.4 = (bf16[128,128]{1,0:T(8,128)(2,1)S(1)}, bf16[128,128]{1,0:T(8,128)(2,1)S(1)}, u32[]{:S(2)}, u32[]{:S(2)}) collective-permute-start(bf16[128,128]{1,0:T(8,128)(2,1)S(1)} %get-tuple-element.28), channel_id=1, source_target_pairs={{0,1},{1,2},{2,3},{3,0},{4,5},{5,6},{6,7},{7,4},{8,9},{9,10},{10,1... | collective-permute-start | bytes 98312 | tf_op jit(solution)/shard_map/ppermute | solution.py:471
  30.9 2.9 %collective-permute-start.2 = (bf16[272,1024]{1,0:T(8,128)(2,1)S(1)}, bf16[272,1024]{1,0:T(8,128)(2,1)}, u32[]{:S(2)}, u32[]{:S(2)}) collective-permute-start(bf16[272,1024]{1,0:T(8,128)(2,1)S(1)} %concatenate.33.refs_1_), channel_id=1, source_target_pairs={{0,4},{4,0},{1,5},{5,1},{2,6},{6,2},{3,7},{7,3},{8,12},{12,8},{9,1... | collective-permute-start | bytes 1671176 | tf_op jit(solution)/shard_map/ppermute | solution.py:489
  33.8 7.4 %collective-permute-done.5 = bf16[128,128]{1,0:T(8,128)(2,1)S(1)} collective-permute-done((bf16[128,128]{1,0:T(8,128)(2,1)S(1)}, bf16[128,128]{1,0:T(8,128)(2,1)S(1)}, u32[]{:S(2)}, u32[]{:S(2)}) %collective-permute-start.5) | collective-permute-done | bytes 32800 | tf_op jit(solution)/shard_map/ppermute | solution.py:471
  41.2 1.4 %broadcast_in_dim.17 = bf16[16,128,384]{2,1,0:T(8,128)(2,1)} broadcast(bf16[128,384]{1,0:T(8,128)(2,1)S(1)} %pad_maximum_fusion.3), dimensions={1,2} | broadcast | bytes 1671168 | tf_op jit(solution)/shard_map/broadcast_in_dim | solution.py:475
  42.6 3.0 %collective-permute-start.7 = (bf16[272,1024]{1,0:T(8,128)(2,1)S(1)}, bf16[272,1024]{1,0:T(8,128)(2,1)}, u32[]{:S(2)}, u32[]{:S(2)}) collective-permute-start(bf16[272,1024]{1,0:T(8,128)(2,1)S(1)} %collective-permute-done.3.refs_3_), channel_id=1, source_target_pairs={{0,4},{4,0},{1,5},{5,1},{2,6},{6,2},{3,7},{7,3},{8,12},{12,8},{9,1... | collective-permute-start | bytes 1671176 | tf_op jit(solution)/shard_map/ppermute | solution.py:491
  45.6 6.7 %all-to-all-start.1 = ((bf16[16,128,384]{2,1,0:T(8,128)(2,1)}), bf16[16,128,384]{2,1,0:T(8,128)(2,1)}, u32[]{:S(2)}, u32[]{:S(2)}) async-start(bf16[16,128,384]{2,1,0:T(8,128)(2,1)} %broadcast_in_dim.17), calls=%async_computation.1 | async-start | bytes 3145728 | tf_op jit(solution)/shard_map/all_to_all | solution.py:497
  52.4 9.3 %shard_map.86.refs_5_ = f32[16,512]{1,0:T(8,128)S(1)} custom-call(s32[4]{0:T(128)S(1)} %pad_add_fusion.1.place_ref, s32[128]{0:T(128)S(1)} %copy-done.2, bf16[2048,384]{1,0:T(8,128)(2,1)} %bitcast.18.refs_0_, bf16[272,1024]{1,0:T(8,128)(2,1)S(1)} %concatenate.33.refs_1_, bf16[272,1024]{1,0:T(8,128)(2,1)} %collective-permute-done.2.refs_2_, ...), custom_call_target="tpu_custom_call" | custom-call | flops 8589934592 | bytes 4194304 | tf_op jit(solution)/shard_map/pallas_call | solution.py:285
  62.1 1.1 collective-permute-start.9
  63.9 1.3 collective-permute-done.9.refs_7_
  65.2 1.8 %collective-permute-done.10.refs_8_ = f32[16,512]{1,0:T(8,128)S(1)} collective-permute-done((f32[16,512]{1,0:T(8,128)S(1)}, f32[16,512]{1,0:T(8,128)S(1)}, u32[]{:S(2)}, u32[]{:S(2)}) %collective-permute-start.10) | collective-permute-done | bytes 32800 | tf_op jit(solution)/shard_map/ppermute | solution.py:506
  67.7 14.5 %shard_map.87 = (bf16[2048,256]{1,0:T(8,128)(2,1)}, f32[128,1024]{1,0:T(8,128)}, bf16[128,1024]{1,0:T(8,128)(2,1)}, bf16[128,1024]{1,0:T(8,128)(2,1)}, bf16[128,1024]{1,0:T(8,128)(2,1)}) custom-call(s32[4]{0:T(128)} %copy-done.3, s32[128]{0:T(128)} %order_ref.3, bf16[2048,384]{1,0:T(8,128)(2,1)} %bitcast.18.refs_0_, bf16[272,1024]{1,0:T(8,128)(2,1)} %copy-done.1, ...), custom_call_target="tpu_custom_call" | custom-call | flops 4294967296 | bytes 8388608 | tf_op jit(solution)/shard_map/pallas_call | solution.py:306
  82.4 8.6 %all-to-all-start.2 = ((bf16[16,128,256]{2,1,0:T(8,128)(2,1)}), bf16[16,128,256]{2,1,0:T(8,128)(2,1)S(1)}, u32[]{:S(2)}, u32[]{:S(2)}) async-start(bf16[16,128,256]{2,1,0:T(8,128)(2,1)} %bitcast.38), calls=%async_computation.2 | async-start | bytes 2097152 | tf_op jit(solution)/shard_map/all_to_all | solution.py:519
  91.1 2.3 %constant_dynamic-slice_fusion = (bf16[2048,128]{1,0:T(8,128)(2,1)}, bf16[2048,128]{1,0:T(8,128)(2,1)}) fusion(bf16[8192,128]{1,0:T(8,128)(2,1)} %param.9, s32[]{:T(128)S(6)} %select_n.118, bf16[8192,128]{1,0:T(8,128)(2,1)} %param.8), kind=kLoop, calls=%fused_computation.45 | loop fusion | bytes 2097156 | tf_op jit(solution)/shard_map/dynamic_slice | solution.py:516
  93.4 1.3 %collective-permute-start.14 = (bf16[128,1024]{1,0:T(8,128)(2,1)}, bf16[128,1024]{1,0:T(8,128)(2,1)}, u32[]{:S(2)}, u32[]{:S(2)}) collective-permute-start(bf16[128,1024]{1,0:T(8,128)(2,1)} %get-tuple-element.23), channel_id=1, source_target_pairs={{0,36},{4,32},{32,4},{36,0},{1,37},{5,33},{33,5},{37,1},{2,38},{6,... | collective-permute-start | bytes 786440 | tf_op jit(solution)/shard_map/ppermute | solution.py:546
  95.6 10.6 %all-to-all-done.2.parts_ref = bf16[16,128,256]{2,1,0:T(8,128)(2,1)S(1)} async-done(((bf16[16,128,256]{2,1,0:T(8,128)(2,1)}), bf16[16,128,256]{2,1,0:T(8,128)(2,1)S(1)}, u32[]{:S(2)}, u32[]{:S(2)}) %all-to-all-start.2) | async-done | bytes 1048608 | tf_op jit(solution)/shard_map/all_to_all | solution.py:519
  106.2 1.4 %shard_map.88 = bf16[16,32,256]{2,1,0:T(8,128)(2,1)} custom-call(s32[3]{0:T(128)S(1)} %pad_add_fusion.place_ref, bf16[16,128,256]{2,1,0:T(8,128)(2,1)S(1)} %all-to-all-done.2.parts_ref, f32[128,128]{1,0:T(8,128)S(1)} %get-tuple-element.47.cos_ref, f32[128,128]{1,0:T(8,128)S(1)} %get-tuple-element.48.sin_ref), custom_call_target="tpu_custom_call" | custom-call | flops 655360 | bytes 2097152 | tf_op jit(solution)/shard_map/pallas_call | solution.py:355
  107.6 8.5 %all-to-all-start.3 = ((bf16[16,32,256]{2,1,0:T(8,128)(2,1)}), bf16[16,32,256]{2,1,0:T(8,128)(2,1)S(1)}, u32[]{:S(2)}, u32[]{:S(2)}) async-start(bf16[16,32,256]{2,1,0:T(8,128)(2,1)} %shard_map.88), calls=%async_computation.3 | async-start | bytes 524288 | tf_op jit(solution)/shard_map/all_to_all | solution.py:539
  116.1 1.4 %pad_maximum_fusion.own_ref = bf16[2048,256]{1,0:T(8,128)(2,1)S(1)} fusion(bf16[2048,128]{1,0:T(8,128)(2,1)} %get-tuple-element.49, bf16[2048,128]{1,0:T(8,128)(2,1)} %get-tuple-element.50), kind=kLoop, calls=%fused_computation.1 | loop fusion | flops 2097152 | bytes 2097152 | tf_op jit(solution)/shard_map/concatenate | solution.py:515
  117.5 2.0 %add_convert_fusion = bf16[128,1024]{1,0:T(8,128)(2,1)} fusion(bf16[128,1024]{1,0:T(8,128)(2,1)} %collective-permute-done.14, bf16[128,1024]{1,0:T(8,128)(2,1)} %collective-permute-done.13, f32[128,1024]{1,0:T(8,128)S(1)} %copy-done.7, bf16[128,1024]{1,0:T(8,128)(2,1)} %collective-permute-done.12), kind=kLoop, calls=%fused_computation.2 | loop fusion | flops 917504 | bytes 1572864 | tf_op jit(solution)/shard_map/convert_element_type | solution.py:548
  119.5 8.2 %all-to-all-done.3.back_ref = bf16[16,32,256]{2,1,0:T(8,128)(2,1)S(1)} async-done(((bf16[16,32,256]{2,1,0:T(8,128)(2,1)}), bf16[16,32,256]{2,1,0:T(8,128)(2,1)S(1)}, u32[]{:S(2)}, u32[]{:S(2)}) %all-to-all-start.3) | async-done | bytes 262176 | tf_op jit(solution)/shard_map/all_to_all | solution.py:539
  127.7 4.1 %shard_map.89 = bf16[128,2048]{1,0:T(8,128)(2,1)} custom-call(s32[3]{0:T(128)S(1)} %pad_add_fusion.place_ref, bf16[16,32,256]{2,1,0:T(8,128)(2,1)S(1)} %all-to-all-done.3.back_ref, bf16[2048,256]{1,0:T(8,128)(2,1)S(1)} %pad_maximum_fusion.own_ref, bf16[2048,384]{1,0:T(8,128)(2,1)} %bitcast.23.mine_ref, bf16[2048,384]{1,0:T(8,128)(2,1)} %collective-permute-done.11.other_ref), custom_call_target="tpu_custom_call" | custom-call | flops 402653184 | bytes 5242880 | tf_op jit(solution)/shard_map/pallas_call | solution.py:402
  (71 shorter events, 6.1 us)
Async XLA Ops:
  0.6 1.7 %copy-start = (bf16[128,8192]{1,0:T(8,128)(2,1)S(1)}, bf16[128,8192]{1,0:T(8,128)(2,1)}, u32[]{:S(2)}) copy-start(bf16[128,8192]{1,0:T(8,128)(2,1)} %param.7) | copy-start | bytes 6291460
  2.3 2.4 %copy-start.6 = (bf16[8192,128]{1,0:T(8,128)(2,1)S(1)}, bf16[8192,128]{1,0:T(8,128)(2,1)}, u32[]{:S(2)}) copy-start(bf16[8192,128]{1,0:T(8,128)(2,1)} %param.8) | copy-start | bytes 6291460
  6.3 4.2 %collective-permute-start = (bf16[2,2,16,384]{3,2,1,0:T(8,128)(2,1)S(1)}, bf16[2,2,16,384]{3,2,1,0:T(8,128)(2,1)S(1)}, u32[]{:S(2)}, u32[]{:S(2)}) collective-permute-start(bf16[2,2,16,384]{3,2,1,0:T(8,128)(2,1)S(1)} %get-tuple-element.35), channel_id=1, source_target_pairs={{0,4},{4,0},{1,5},{5,1},{2,6},{6,2},{3,7},{7,3},{8,12},{12,8},{9,1... | collective-permute-start | bytes 147464 | tf_op jit(solution)/shard_map/ppermute | solution.py:453
  10.5 3.0 %collective-permute-start.1 = (bf16[2,2,16,384]{3,2,1,0:T(8,128)(2,1)S(1)}, bf16[2,2,16,384]{3,2,1,0:T(8,128)(2,1)S(1)}, u32[]{:S(2)}, u32[]{:S(2)}) collective-permute-start(bf16[2,2,16,384]{3,2,1,0:T(8,128)(2,1)S(1)} %get-tuple-element.34), channel_id=1, source_target_pairs={{0,32},{32,0},{1,33},{33,1},{2,34},{34,2},{3,35},{35,3},{4,36},{36... | collective-permute-start | bytes 147464 | tf_op jit(solution)/shard_map/ppermute | solution.py:456
  13.6 6.7 %copy-start.13 = (s32[128]{0:T(128)S(1)}, s32[128]{0:T(128)}, u32[]{:S(2)}) copy-start(s32[128]{0:T(128)} %param.12) | copy-start | bytes 1540
  13.6 6.9 %copy-start.8 = (bf16[128,1024]{1,0:T(8,128)(2,1)S(1)}, bf16[128,1024]{1,0:T(8,128)(2,1)}, u32[]{:S(2)}) copy-start(bf16[128,1024]{1,0:T(8,128)(2,1)} %param.10) | copy-start | bytes 786436
  13.6 6.9 %copy-start.9 = (bf16[128,1024]{1,0:T(8,128)(2,1)S(1)}, bf16[128,1024]{1,0:T(8,128)(2,1)}, u32[]{:S(2)}) copy-start(bf16[128,1024]{1,0:T(8,128)(2,1)} %param.11) | copy-start | bytes 786436
  15.0 30.6 %all-to-all-start = ((bf16[16,128,384]{2,1,0:T(8,128)(2,1)}), bf16[16,128,384]{2,1,0:T(8,128)(2,1)}, u32[]{:S(2)}, u32[]{:S(2)}) async-start(bf16[16,128,384]{2,1,0:T(8,128)(2,1)} %broadcast_in_dim.13), calls=%async_computation | async-start | bytes 3145728 | tf_op jit(solution)/shard_map/all_to_all | solution.py:494
  20.9 31.4 %copy-start.1 = (bf16[272,1024]{1,0:T(8,128)(2,1)}, bf16[272,1024]{1,0:T(8,128)(2,1)S(1)}, u32[]{:S(2)}) copy-start(bf16[272,1024]{1,0:T(8,128)(2,1)S(1)} %concatenate.33.refs_1_) | copy-start | bytes 1671172
  20.9 20.3 %collective-permute-start.3 = (bf16[272,1024]{1,0:T(8,128)(2,1)S(1)}, bf16[272,1024]{1,0:T(8,128)(2,1)S(1)}, u32[]{:S(2)}, u32[]{:S(2)}) collective-permute-start(bf16[272,1024]{1,0:T(8,128)(2,1)S(1)} %concatenate.33.refs_1_), channel_id=1, source_target_pairs={{0,32},{32,0},{1,33},{33,1},{2,34},{34,2},{3,35},{35,3},{4,36},{36... | collective-permute-start | bytes 1671176 | tf_op jit(solution)/shard_map/ppermute | solution.py:485
  22.5 11.4 %collective-permute-start.6 = (bf16[128,128]{1,0:T(8,128)(2,1)S(1)}, bf16[128,128]{1,0:T(8,128)(2,1)S(1)}, u32[]{:S(2)}, u32[]{:S(2)}) collective-permute-start(bf16[128,128]{1,0:T(8,128)(2,1)S(1)} %get-tuple-element.29), channel_id=1, source_target_pairs={{0,3},{1,0},{2,1},{3,2},{4,7},{5,4},{6,5},{7,6},{8,11},{9,8},{10,9... | collective-permute-start | bytes 98312 | tf_op jit(solution)/shard_map/ppermute | solution.py:471
  27.7 13.5 %collective-permute-start.5 = (bf16[128,128]{1,0:T(8,128)(2,1)S(1)}, bf16[128,128]{1,0:T(8,128)(2,1)S(1)}, u32[]{:S(2)}, u32[]{:S(2)}) collective-permute-start(bf16[128,128]{1,0:T(8,128)(2,1)S(1)} %get-tuple-element.30), channel_id=1, source_target_pairs={{0,2},{1,3},{2,0},{3,1},{4,6},{5,7},{6,4},{7,5},{8,10},{9,11},{10,... | collective-permute-start | bytes 98312 | tf_op jit(solution)/shard_map/ppermute | solution.py:471
  28.8 12.4 %collective-permute-start.4 = (bf16[128,128]{1,0:T(8,128)(2,1)S(1)}, bf16[128,128]{1,0:T(8,128)(2,1)S(1)}, u32[]{:S(2)}, u32[]{:S(2)}) collective-permute-start(bf16[128,128]{1,0:T(8,128)(2,1)S(1)} %get-tuple-element.28), channel_id=1, source_target_pairs={{0,1},{1,2},{2,3},{3,0},{4,5},{5,6},{6,7},{7,4},{8,9},{9,10},{10,1... | collective-permute-start | bytes 98312 | tf_op jit(solution)/shard_map/ppermute | solution.py:471
  30.9 21.4 %collective-permute-start.2 = (bf16[272,1024]{1,0:T(8,128)(2,1)S(1)}, bf16[272,1024]{1,0:T(8,128)(2,1)}, u32[]{:S(2)}, u32[]{:S(2)}) collective-permute-start(bf16[272,1024]{1,0:T(8,128)(2,1)S(1)} %concatenate.33.refs_1_), channel_id=1, source_target_pairs={{0,4},{4,0},{1,5},{5,1},{2,6},{6,2},{3,7},{7,3},{8,12},{12,8},{9,1... | collective-permute-start | bytes 1671176 | tf_op jit(solution)/shard_map/ppermute | solution.py:489
  41.2 11.1 %copy-start.2 = (s32[128]{0:T(128)S(1)}, s32[128]{0:T(128)}, u32[]{:S(2)}) copy-start(s32[128]{0:T(128)} %order_ref.3) | copy-start | bytes 1540
  41.2 11.1 %copy-start.4 = (bf16[272,1024]{1,0:T(8,128)(2,1)}, bf16[272,1024]{1,0:T(8,128)(2,1)S(1)}, u32[]{:S(2)}) copy-start(bf16[272,1024]{1,0:T(8,128)(2,1)S(1)} %collective-permute-done.3.refs_3_) | copy-start | bytes 1671172
  42.6 9.7 %collective-permute-start.7 = (bf16[272,1024]{1,0:T(8,128)(2,1)S(1)}, bf16[272,1024]{1,0:T(8,128)(2,1)}, u32[]{:S(2)}, u32[]{:S(2)}) collective-permute-start(bf16[272,1024]{1,0:T(8,128)(2,1)S(1)} %collective-permute-done.3.refs_3_), channel_id=1, source_target_pairs={{0,4},{4,0},{1,5},{5,1},{2,6},{6,2},{3,7},{7,3},{8,12},{12,8},{9,1... | collective-permute-start | bytes 1671176 | tf_op jit(solution)/shard_map/ppermute | solution.py:491
  45.6 36.6 %all-to-all-start.1 = ((bf16[16,128,384]{2,1,0:T(8,128)(2,1)}), bf16[16,128,384]{2,1,0:T(8,128)(2,1)}, u32[]{:S(2)}, u32[]{:S(2)}) async-start(bf16[16,128,384]{2,1,0:T(8,128)(2,1)} %broadcast_in_dim.17), calls=%async_computation.1 | async-start | bytes 3145728 | tf_op jit(solution)/shard_map/all_to_all | solution.py:497
  52.3 9.4 %copy-start.3 = (s32[4]{0:T(128)}, s32[4]{0:T(128)S(1)}, u32[]{:S(2)}) copy-start(s32[4]{0:T(128)S(1)} %pad_add_fusion.1.place_ref) | copy-start | bytes 52
  61.7 5.4 %copy-start.5 = (f32[16,512]{1,0:T(8,128)}, f32[16,512]{1,0:T(8,128)S(1)}, u32[]{:S(2)}) copy-start(f32[16,512]{1,0:T(8,128)S(1)} %shard_map.86.refs_5_) | copy-start | bytes 98308
  61.7 2.2 %collective-permute-start.8 = (f32[16,512]{1,0:T(8,128)S(1)}, f32[16,512]{1,0:T(8,128)S(1)}, u32[]{:S(2)}, u32[]{:S(2)}) collective-permute-start(f32[16,512]{1,0:T(8,128)S(1)} %shard_map.86.refs_5_), channel_id=1, source_target_pairs={{0,4},{4,0},{1,5},{5,1},{2,6},{6,2},{3,7},{7,3},{8,12},{12,8},{9,1... | collective-permute-start | bytes 98312 | tf_op jit(solution)/shard_map/ppermute | solution.py:504
  62.1 3.2 %collective-permute-start.9 = (f32[16,512]{1,0:T(8,128)S(1)}, f32[16,512]{1,0:T(8,128)S(1)}, u32[]{:S(2)}, u32[]{:S(2)}) collective-permute-start(f32[16,512]{1,0:T(8,128)S(1)} %shard_map.86.refs_5_), channel_id=1, source_target_pairs={{0,32},{32,0},{1,33},{33,1},{2,34},{34,2},{3,35},{35,3},{4,36},{36... | collective-permute-start | bytes 98312 | tf_op jit(solution)/shard_map/ppermute | solution.py:505
  63.1 3.9 %collective-permute-start.10 = (f32[16,512]{1,0:T(8,128)S(1)}, f32[16,512]{1,0:T(8,128)S(1)}, u32[]{:S(2)}, u32[]{:S(2)}) collective-permute-start(f32[16,512]{1,0:T(8,128)S(1)} %shard_map.86.refs_5_), channel_id=1, source_target_pairs={{0,36},{4,32},{32,4},{36,0},{1,37},{5,33},{33,5},{37,1},{2,38},{6,... | collective-permute-start | bytes 98312 | tf_op jit(solution)/shard_map/ppermute | solution.py:506
  63.9 3.1 %copy-start.10 = (f32[16,512]{1,0:T(8,128)}, f32[16,512]{1,0:T(8,128)S(1)}, u32[]{:S(2)}) copy-start(f32[16,512]{1,0:T(8,128)S(1)} %collective-permute-done.8.refs_6_) | copy-start | bytes 98308
  65.2 1.8 %copy-start.11 = (f32[16,512]{1,0:T(8,128)}, f32[16,512]{1,0:T(8,128)S(1)}, u32[]{:S(2)}) copy-start(f32[16,512]{1,0:T(8,128)S(1)} %collective-permute-done.9.refs_7_) | copy-start | bytes 98308
  82.2 45.5 %collective-permute-start.11 = (bf16[2048,384]{1,0:T(8,128)(2,1)}, bf16[2048,384]{1,0:T(8,128)(2,1)}, u32[]{:S(2)}, u32[]{:S(2)}) collective-permute-start(bf16[2048,384]{1,0:T(8,128)(2,1)} %bitcast.23.mine_ref), channel_id=1, source_target_pairs={{0,4},{4,0},{1,5},{5,1},{2,6},{6,2},{3,7},{7,3},{8,12},{12,8},{9,1... | collective-permute-start | bytes 4718600 | tf_op jit(solution)/shard_map/ppermute | solution.py:513
  82.4 23.8 %all-to-all-start.2 = ((bf16[16,128,256]{2,1,0:T(8,128)(2,1)}), bf16[16,128,256]{2,1,0:T(8,128)(2,1)S(1)}, u32[]{:S(2)}, u32[]{:S(2)}) async-start(bf16[16,128,256]{2,1,0:T(8,128)(2,1)} %bitcast.38), calls=%async_computation.2 | async-start | bytes 2097152 | tf_op jit(solution)/shard_map/all_to_all | solution.py:519
  93.4 24.1 %collective-permute-start.14 = (bf16[128,1024]{1,0:T(8,128)(2,1)}, bf16[128,1024]{1,0:T(8,128)(2,1)}, u32[]{:S(2)}, u32[]{:S(2)}) collective-permute-start(bf16[128,1024]{1,0:T(8,128)(2,1)} %get-tuple-element.23), channel_id=1, source_target_pairs={{0,36},{4,32},{32,4},{36,0},{1,37},{5,33},{33,5},{37,1},{2,38},{6,... | collective-permute-start | bytes 786440 | tf_op jit(solution)/shard_map/ppermute | solution.py:546
  94.7 22.8 %collective-permute-start.13 = (bf16[128,1024]{1,0:T(8,128)(2,1)}, bf16[128,1024]{1,0:T(8,128)(2,1)}, u32[]{:S(2)}, u32[]{:S(2)}) collective-permute-start(bf16[128,1024]{1,0:T(8,128)(2,1)} %get-tuple-element.22), channel_id=1, source_target_pairs={{0,32},{32,0},{1,33},{33,1},{2,34},{34,2},{3,35},{35,3},{4,36},{36... | collective-permute-start | bytes 786440 | tf_op jit(solution)/shard_map/ppermute | solution.py:545
  95.5 22.1 %collective-permute-start.12 = (bf16[128,1024]{1,0:T(8,128)(2,1)}, bf16[128,1024]{1,0:T(8,128)(2,1)}, u32[]{:S(2)}, u32[]{:S(2)}) collective-permute-start(bf16[128,1024]{1,0:T(8,128)(2,1)} %get-tuple-element.21), channel_id=1, source_target_pairs={{0,4},{4,0},{1,5},{5,1},{2,6},{6,2},{3,7},{7,3},{8,12},{12,8},{9,1... | collective-permute-start | bytes 786440 | tf_op jit(solution)/shard_map/ppermute | solution.py:544
  107.6 20.1 %all-to-all-start.3 = ((bf16[16,32,256]{2,1,0:T(8,128)(2,1)}), bf16[16,32,256]{2,1,0:T(8,128)(2,1)S(1)}, u32[]{:S(2)}, u32[]{:S(2)}) async-start(bf16[16,32,256]{2,1,0:T(8,128)(2,1)} %shard_map.88), calls=%async_computation.3 | async-start | bytes 524288 | tf_op jit(solution)/shard_map/all_to_all | solution.py:539
  116.1 1.4 %copy-start.7 = (f32[128,1024]{1,0:T(8,128)S(1)}, f32[128,1024]{1,0:T(8,128)}, u32[]{:S(2)}) copy-start(f32[128,1024]{1,0:T(8,128)} %get-tuple-element.20) | copy-start | bytes 1572868
  (1 other events, 0.6 us)

commit v2 on v1

--- a/solution.py
+++ b/solution.py
@@ -14,9 +14,9 @@
 n_ctx = 64
 n_head = 4
 block_len = 64
-key_span = 256
+key_span = 192
 granule = 16
-item_group = 3
+item_group = 4
 log2e = 1.4426950408889634
 
 
@@ -275,7 +275,7 @@
         pltpu.VMEM((4 * rows, head_dim), jnp.bfloat16),
         pltpu.VMEM((8, half), jnp.int32),
         pltpu.VMEM((key_span, half), jnp.int32),
-        pltpu.SMEM((3, 64), jnp.int32),
+        pltpu.SMEM((3, 128), jnp.int32),
     ]
 
 

time: 131 us -> 130 us (level); the launches traced: 132 us -> 128 us
  Pallas kernels: 29.3 us -> 25 us
    pallas_call x1, Pallas kernels: 14.5 us -> 11.9 us  [run_grads(): pl.pallas_call(functools.partial(grads_kernel, factor=scaling * log2e, sc...]
    pallas_call x1, Pallas kernels: 9.3 us -> 7.55 us  [run_stats(): pl.pallas_call(functools.partial(stats_kernel, factor=scaling * log2e), o...]
  transfers between devices with their start and end apart: 19 -> 19, of which waited for: 7 -> 7; matrix products, arithmetic and copies ran while one was open for 7% -> 7% of each run, Pallas kernels for 19% -> 16%
where the time goes in v2:
time: 130 us; the launch traced here: 128 us
  starting transfers between devices  53.7 us (41%)
  waiting for transfers between devices  32.2 us (25%)
  Pallas kernels  25 us (19%)
  local copies, waits for them, and re-layouts  6.83 us (5%)
  other arithmetic  6.49 us (5%)
  matrix products  3.13 us (2%)
    pallas_call x1, Pallas kernels, run_grads(): pl.pallas_call(functools.partial(grads_kernel, factor=scaling * log2e, sc...  11.9 us
    all_to_all x1, waiting for transfers between devices, shards(): lax.all_to_all(grads.reshape(16, row_count, 2 * head_dim), ('x', 'y'), 0, 0)  10.6 us
    all_to_all x1, starting transfers between devices, shards(): lax.all_to_all(grads.reshape(16, row_count, 2 * head_dim), ('x', 'y'), 0, 0)  9.64 us
    ppermute x3, starting transfers between devices, shards(): lax.ppermute(pick(weight_shares, (head + s) % n_head, 0), 'head', head_pe...  8.45 us
    all_to_all x1, starting transfers between devices, shards(): back = lax.all_to_all(back, ('zl', 'core', 'head'), 0, 0)  8.41 us
    all_to_all x1, waiting for transfers between devices, shards(): back = lax.all_to_all(back, ('zl', 'core', 'head'), 0, 0)  8.22 us
    pallas_call x1, Pallas kernels, run_stats(): pl.pallas_call(functools.partial(stats_kernel, factor=scaling * log2e), o...  7.55 us
    ppermute x3, waiting for transfers between devices, shards(): lax.ppermute(pick(weight_shares, (head + s) % n_head, 0), 'head', head_pe...  7.39 us
  transfers between devices with their start and end apart: 19, of which 7 were waited for; matrix products, arithmetic and copies ran while one was open for 7% of the time, Pallas kernels for 16%

profile of v2, /device:TPU:1, one launch (start us, length us, event | category | flops | bytes accessed | tf_op | source)
XLA Modules:
  0.0 128.5 jit_solution(7502710576119361929)
XLA Ops:
  0.7 0.9 broadcast_multiply_fusion
  2.3 2.4 %convolution_convert_fusion = bf16[128,128]{1,0:T(8,128)(2,1)S(1)} fusion(bf16[128,8192]{1,0:T(8,128)(2,1)S(1)} %copy-done, bf16[8192,128]{1,0:T(8,128)(2,1)} %param.9), kind=kOutput, calls=%fused_computation | convolution fusion | flops 268451840 | bytes 4227072 | tf_op jit(solution)/shard_map/dot_general | solution.py:447
  6.3 3.3 %collective-permute-start = (bf16[2,2,16,384]{3,2,1,0:T(8,128)(2,1)S(1)}, bf16[2,2,16,384]{3,2,1,0:T(8,128)(2,1)S(1)}, u32[]{:S(2)}, u32[]{:S(2)}) collective-permute-start(bf16[2,2,16,384]{3,2,1,0:T(8,128)(2,1)S(1)} %get-tuple-element.35), channel_id=1, source_target_pairs={{0,4},{4,0},{1,5},{5,1},{2,6},{6,2},{3,7},{7,3},{8,12},{12,8},{9,1... | collective-permute-start | bytes 147464 | tf_op jit(solution)/shard_map/ppermute | solution.py:453
  9.6 0.9 collective-permute-done
  10.6 1.0 select_bitcast_fusion
  11.6 1.9 %collective-permute-done.1 = bf16[2,2,16,384]{3,2,1,0:T(8,128)(2,1)S(1)} collective-permute-done((bf16[2,2,16,384]{3,2,1,0:T(8,128)(2,1)S(1)}, bf16[2,2,16,384]{3,2,1,0:T(8,128)(2,1)S(1)}, u32[]{:S(2)}, u32[]{:S(2)}) %collective-permute-start.1) | collective-permute-done | bytes 49184 | tf_op jit(solution)/shard_map/ppermute | solution.py:456
  13.6 1.4 %broadcast_in_dim.13 = bf16[16,128,384]{2,1,0:T(8,128)(2,1)} broadcast(bf16[128,384]{1,0:T(8,128)(2,1)S(1)} %bitcast.40), dimensions={1,2} | broadcast | bytes 1671168 | tf_op jit(solution)/shard_map/broadcast_in_dim | solution.py:495
  15.0 5.2 %all-to-all-start = ((bf16[16,128,384]{2,1,0:T(8,128)(2,1)}), bf16[16,128,384]{2,1,0:T(8,128)(2,1)}, u32[]{:S(2)}, u32[]{:S(2)}) async-start(bf16[16,128,384]{2,1,0:T(8,128)(2,1)} %broadcast_in_dim.13), calls=%async_computation | async-start | bytes 3145728 | tf_op jit(solution)/shard_map/all_to_all | solution.py:494
  20.9 1.5 %collective-permute-start.3 = (bf16[272,1024]{1,0:T(8,128)(2,1)S(1)}, bf16[272,1024]{1,0:T(8,128)(2,1)S(1)}, u32[]{:S(2)}, u32[]{:S(2)}) collective-permute-start(bf16[272,1024]{1,0:T(8,128)(2,1)S(1)} %concatenate.33.refs_1_), channel_id=1, source_target_pairs={{0,32},{32,0},{1,33},{33,1},{2,34},{34,2},{3,35},{35,3},{4,36},{36... | collective-permute-start | bytes 1671176 | tf_op jit(solution)/shard_map/ppermute | solution.py:485
  22.5 5.2 %collective-permute-start.6 = (bf16[128,128]{1,0:T(8,128)(2,1)S(1)}, bf16[128,128]{1,0:T(8,128)(2,1)S(1)}, u32[]{:S(2)}, u32[]{:S(2)}) collective-permute-start(bf16[128,128]{1,0:T(8,128)(2,1)S(1)} %get-tuple-element.29), channel_id=1, source_target_pairs={{0,3},{1,0},{2,1},{3,2},{4,7},{5,4},{6,5},{7,6},{8,11},{9,8},{10,9... | collective-permute-start | bytes 98312 | tf_op jit(solution)/shard_map/ppermute | solution.py:471
  27.7 1.2 collective-permute-start.5
  28.8 2.1 %collective-permute-start.4 = (bf16[128,128]{1,0:T(8,128)(2,1)S(1)}, bf16[128,128]{1,0:T(8,128)(2,1)S(1)}, u32[]{:S(2)}, u32[]{:S(2)}) collective-permute-start(bf16[128,128]{1,0:T(8,128)(2,1)S(1)} %get-tuple-element.28), channel_id=1, source_target_pairs={{0,1},{1,2},{2,3},{3,0},{4,5},{5,6},{6,7},{7,4},{8,9},{9,10},{10,1... | collective-permute-start | bytes 98312 | tf_op jit(solution)/shard_map/ppermute | solution.py:471
  30.9 2.9 %collective-permute-start.2 = (bf16[272,1024]{1,0:T(8,128)(2,1)S(1)}, bf16[272,1024]{1,0:T(8,128)(2,1)}, u32[]{:S(2)}, u32[]{:S(2)}) collective-permute-start(bf16[272,1024]{1,0:T(8,128)(2,1)S(1)} %concatenate.33.refs_1_), channel_id=1, source_target_pairs={{0,4},{4,0},{1,5},{5,1},{2,6},{6,2},{3,7},{7,3},{8,12},{12,8},{9,1... | collective-permute-start | bytes 1671176 | tf_op jit(solution)/shard_map/ppermute | solution.py:489
  33.8 7.4 %collective-permute-done.5 = bf16[128,128]{1,0:T(8,128)(2,1)S(1)} collective-permute-done((bf16[128,128]{1,0:T(8,128)(2,1)S(1)}, bf16[128,128]{1,0:T(8,128)(2,1)S(1)}, u32[]{:S(2)}, u32[]{:S(2)}) %collective-permute-start.5) | collective-permute-done | bytes 32800 | tf_op jit(solution)/shard_map/ppermute | solution.py:471
  41.2 1.4 %broadcast_in_dim.17 = bf16[16,128,384]{2,1,0:T(8,128)(2,1)} broadcast(bf16[128,384]{1,0:T(8,128)(2,1)S(1)} %pad_maximum_fusion.3), dimensions={1,2} | broadcast | bytes 1671168 | tf_op jit(solution)/shard_map/broadcast_in_dim | solution.py:475
  42.6 3.0 %collective-permute-start.7 = (bf16[272,1024]{1,0:T(8,128)(2,1)S(1)}, bf16[272,1024]{1,0:T(8,128)(2,1)}, u32[]{:S(2)}, u32[]{:S(2)}) collective-permute-start(bf16[272,1024]{1,0:T(8,128)(2,1)S(1)} %collective-permute-done.3.refs_3_), channel_id=1, source_target_pairs={{0,4},{4,0},{1,5},{5,1},{2,6},{6,2},{3,7},{7,3},{8,12},{12,8},{9,1... | collective-permute-start | bytes 1671176 | tf_op jit(solution)/shard_map/ppermute | solution.py:491
  45.6 6.7 %all-to-all-start.1 = ((bf16[16,128,384]{2,1,0:T(8,128)(2,1)}), bf16[16,128,384]{2,1,0:T(8,128)(2,1)}, u32[]{:S(2)}, u32[]{:S(2)}) async-start(bf16[16,128,384]{2,1,0:T(8,128)(2,1)} %broadcast_in_dim.17), calls=%async_computation.1 | async-start | bytes 3145728 | tf_op jit(solution)/shard_map/all_to_all | solution.py:497
  52.4 7.6 %shard_map.86.refs_5_ = f32[16,512]{1,0:T(8,128)S(1)} custom-call(s32[4]{0:T(128)S(1)} %pad_add_fusion.1.place_ref, s32[128]{0:T(128)S(1)} %copy-done.2, bf16[2048,384]{1,0:T(8,128)(2,1)} %bitcast.18.refs_0_, bf16[272,1024]{1,0:T(8,128)(2,1)S(1)} %concatenate.33.refs_1_, bf16[272,1024]{1,0:T(8,128)(2,1)} %collective-permute-done.2.refs_2_, ...), custom_call_target="tpu_custom_call" | custom-call | flops 8589934592 | bytes 4194304 | tf_op jit(solution)/shard_map/pallas_call | solution.py:285
  60.3 1.1 collective-permute-start.9
  62.2 1.3 %collective-permute-done.9.refs_7_ = f32[16,512]{1,0:T(8,128)S(1)} collective-permute-done((f32[16,512]{1,0:T(8,128)S(1)}, f32[16,512]{1,0:T(8,128)S(1)}, u32[]{:S(2)}, u32[]{:S(2)}) %collective-permute-start.9) | collective-permute-done | bytes 32800 | tf_op jit(solution)/shard_map/ppermute | solution.py:505
  63.5 1.8 %collective-permute-done.10.refs_8_ = f32[16,512]{1,0:T(8,128)S(1)} collective-permute-done((f32[16,512]{1,0:T(8,128)S(1)}, f32[16,512]{1,0:T(8,128)S(1)}, u32[]{:S(2)}, u32[]{:S(2)}) %collective-permute-start.10) | collective-permute-done | bytes 32800 | tf_op jit(solution)/shard_map/ppermute | solution.py:506
  65.9 11.9 %shard_map.87 = (bf16[2048,256]{1,0:T(8,128)(2,1)}, f32[128,1024]{1,0:T(8,128)}, bf16[128,1024]{1,0:T(8,128)(2,1)}, bf16[128,1024]{1,0:T(8,128)(2,1)}, bf16[128,1024]{1,0:T(8,128)(2,1)}) custom-call(s32[4]{0:T(128)} %copy-done.3, s32[128]{0:T(128)} %order_ref.3, bf16[2048,384]{1,0:T(8,128)(2,1)} %bitcast.18.refs_0_, bf16[272,1024]{1,0:T(8,128)(2,1)} %copy-done.1, ...), custom_call_target="tpu_custom_call" | custom-call | flops 4294967296 | bytes 8388608 | tf_op jit(solution)/shard_map/pallas_call | solution.py:306
  78.0 9.6 %all-to-all-start.2 = ((bf16[16,128,256]{2,1,0:T(8,128)(2,1)}), bf16[16,128,256]{2,1,0:T(8,128)(2,1)S(1)}, u32[]{:S(2)}, u32[]{:S(2)}) async-start(bf16[16,128,256]{2,1,0:T(8,128)(2,1)} %bitcast.38), calls=%async_computation.2 | async-start | bytes 2097152 | tf_op jit(solution)/shard_map/all_to_all | solution.py:519
  87.8 2.3 %constant_dynamic-slice_fusion = (bf16[2048,128]{1,0:T(8,128)(2,1)}, bf16[2048,128]{1,0:T(8,128)(2,1)}) fusion(bf16[8192,128]{1,0:T(8,128)(2,1)} %param.9, s32[]{:T(128)S(6)} %select_n.118, bf16[8192,128]{1,0:T(8,128)(2,1)} %param.8), kind=kLoop, calls=%fused_computation.45 | loop fusion | bytes 2097156 | tf_op jit(solution)/shard_map/dynamic_slice | solution.py:516
  90.0 1.3 collective-permute-start.14
  92.2 10.6 %all-to-all-done.2.parts_ref = bf16[16,128,256]{2,1,0:T(8,128)(2,1)S(1)} async-done(((bf16[16,128,256]{2,1,0:T(8,128)(2,1)}), bf16[16,128,256]{2,1,0:T(8,128)(2,1)S(1)}, u32[]{:S(2)}, u32[]{:S(2)}) %all-to-all-start.2) | async-done | bytes 1048608 | tf_op jit(solution)/shard_map/all_to_all | solution.py:519
  102.9 1.4 %shard_map.88 = bf16[16,32,256]{2,1,0:T(8,128)(2,1)} custom-call(s32[3]{0:T(128)S(1)} %pad_add_fusion.place_ref, bf16[16,128,256]{2,1,0:T(8,128)(2,1)S(1)} %all-to-all-done.2.parts_ref, f32[128,128]{1,0:T(8,128)S(1)} %get-tuple-element.47.cos_ref, f32[128,128]{1,0:T(8,128)S(1)} %get-tuple-element.48.sin_ref), custom_call_target="tpu_custom_call" | custom-call | flops 655360 | bytes 2097152 | tf_op jit(solution)/shard_map/pallas_call | solution.py:355
  104.3 8.4 %all-to-all-start.3 = ((bf16[16,32,256]{2,1,0:T(8,128)(2,1)}), bf16[16,32,256]{2,1,0:T(8,128)(2,1)S(1)}, u32[]{:S(2)}, u32[]{:S(2)}) async-start(bf16[16,32,256]{2,1,0:T(8,128)(2,1)} %shard_map.88), calls=%async_computation.3 | async-start | bytes 524288 | tf_op jit(solution)/shard_map/all_to_all | solution.py:539
  112.7 1.4 %pad_maximum_fusion.own_ref = bf16[2048,256]{1,0:T(8,128)(2,1)S(1)} fusion(bf16[2048,128]{1,0:T(8,128)(2,1)} %get-tuple-element.49, bf16[2048,128]{1,0:T(8,128)(2,1)} %get-tuple-element.50), kind=kLoop, calls=%fused_computation.1 | loop fusion | flops 2097152 | bytes 2097152 | tf_op jit(solution)/shard_map/concatenate | solution.py:515
  114.2 2.0 %add_convert_fusion = bf16[128,1024]{1,0:T(8,128)(2,1)} fusion(bf16[128,1024]{1,0:T(8,128)(2,1)} %collective-permute-done.14, bf16[128,1024]{1,0:T(8,128)(2,1)} %collective-permute-done.13, f32[128,1024]{1,0:T(8,128)S(1)} %copy-done.7, bf16[128,1024]{1,0:T(8,128)(2,1)} %collective-permute-done.12), kind=kLoop, calls=%fused_computation.2 | loop fusion | flops 917504 | bytes 1572864 | tf_op jit(solution)/shard_map/convert_element_type | solution.py:548
  116.1 8.2 %all-to-all-done.3.back_ref = bf16[16,32,256]{2,1,0:T(8,128)(2,1)S(1)} async-done(((bf16[16,32,256]{2,1,0:T(8,128)(2,1)}), bf16[16,32,256]{2,1,0:T(8,128)(2,1)S(1)}, u32[]{:S(2)}, u32[]{:S(2)}) %all-to-all-start.3) | async-done | bytes 262176 | tf_op jit(solution)/shard_map/all_to_all | solution.py:539
  124.3 4.1 %shard_map.89 = bf16[128,2048]{1,0:T(8,128)(2,1)} custom-call(s32[3]{0:T(128)S(1)} %pad_add_fusion.place_ref, bf16[16,32,256]{2,1,0:T(8,128)(2,1)S(1)} %all-to-all-done.3.back_ref, bf16[2048,256]{1,0:T(8,128)(2,1)S(1)} %pad_maximum_fusion.own_ref, bf16[2048,384]{1,0:T(8,128)(2,1)} %bitcast.23.mine_ref, bf16[2048,384]{1,0:T(8,128)(2,1)} %collective-permute-done.11.other_ref), custom_call_target="tpu_custom_call" | custom-call | flops 402653184 | bytes 5242880 | tf_op jit(solution)/shard_map/pallas_call | solution.py:402
  (71 shorter events, 6.0 us)
Async XLA Ops:
  0.6 1.7 %copy-start = (bf16[128,8192]{1,0:T(8,128)(2,1)S(1)}, bf16[128,8192]{1,0:T(8,128)(2,1)}, u32[]{:S(2)}) copy-start(bf16[128,8192]{1,0:T(8,128)(2,1)} %param.7) | copy-start | bytes 6291460
  2.3 2.4 %copy-start.6 = (bf16[8192,128]{1,0:T(8,128)(2,1)S(1)}, bf16[8192,128]{1,0:T(8,128)(2,1)}, u32[]{:S(2)}) copy-start(bf16[8192,128]{1,0:T(8,128)(2,1)} %param.8) | copy-start | bytes 6291460
  6.3 4.2 %collective-permute-start = (bf16[2,2,16,384]{3,2,1,0:T(8,128)(2,1)S(1)}, bf16[2,2,16,384]{3,2,1,0:T(8,128)(2,1)S(1)}, u32[]{:S(2)}, u32[]{:S(2)}) collective-permute-start(bf16[2,2,16,384]{3,2,1,0:T(8,128)(2,1)S(1)} %get-tuple-element.35), channel_id=1, source_target_pairs={{0,4},{4,0},{1,5},{5,1},{2,6},{6,2},{3,7},{7,3},{8,12},{12,8},{9,1... | collective-permute-start | bytes 147464 | tf_op jit(solution)/shard_map/ppermute | solution.py:453
  10.5 3.0 %collective-permute-start.1 = (bf16[2,2,16,384]{3,2,1,0:T(8,128)(2,1)S(1)}, bf16[2,2,16,384]{3,2,1,0:T(8,128)(2,1)S(1)}, u32[]{:S(2)}, u32[]{:S(2)}) collective-permute-start(bf16[2,2,16,384]{3,2,1,0:T(8,128)(2,1)S(1)} %get-tuple-element.34), channel_id=1, source_target_pairs={{0,32},{32,0},{1,33},{33,1},{2,34},{34,2},{3,35},{35,3},{4,36},{36... | collective-permute-start | bytes 147464 | tf_op jit(solution)/shard_map/ppermute | solution.py:456
  13.6 6.7 %copy-start.13 = (s32[128]{0:T(128)S(1)}, s32[128]{0:T(128)}, u32[]{:S(2)}) copy-start(s32[128]{0:T(128)} %param.12) | copy-start | bytes 1540
  13.6 6.9 %copy-start.8 = (bf16[128,1024]{1,0:T(8,128)(2,1)S(1)}, bf16[128,1024]{1,0:T(8,128)(2,1)}, u32[]{:S(2)}) copy-start(bf16[128,1024]{1,0:T(8,128)(2,1)} %param.10) | copy-start | bytes 786436
  13.6 6.9 %copy-start.9 = (bf16[128,1024]{1,0:T(8,128)(2,1)S(1)}, bf16[128,1024]{1,0:T(8,128)(2,1)}, u32[]{:S(2)}) copy-start(bf16[128,1024]{1,0:T(8,128)(2,1)} %param.11) | copy-start | bytes 786436
  15.0 30.6 %all-to-all-start = ((bf16[16,128,384]{2,1,0:T(8,128)(2,1)}), bf16[16,128,384]{2,1,0:T(8,128)(2,1)}, u32[]{:S(2)}, u32[]{:S(2)}) async-start(bf16[16,128,384]{2,1,0:T(8,128)(2,1)} %broadcast_in_dim.13), calls=%async_computation | async-start | bytes 3145728 | tf_op jit(solution)/shard_map/all_to_all | solution.py:494
  20.9 31.4 %copy-start.1 = (bf16[272,1024]{1,0:T(8,128)(2,1)}, bf16[272,1024]{1,0:T(8,128)(2,1)S(1)}, u32[]{:S(2)}) copy-start(bf16[272,1024]{1,0:T(8,128)(2,1)S(1)} %concatenate.33.refs_1_) | copy-start | bytes 1671172
  20.9 20.3 %collective-permute-start.3 = (bf16[272,1024]{1,0:T(8,128)(2,1)S(1)}, bf16[272,1024]{1,0:T(8,128)(2,1)S(1)}, u32[]{:S(2)}, u32[]{:S(2)}) collective-permute-start(bf16[272,1024]{1,0:T(8,128)(2,1)S(1)} %concatenate.33.refs_1_), channel_id=1, source_target_pairs={{0,32},{32,0},{1,33},{33,1},{2,34},{34,2},{3,35},{35,3},{4,36},{36... | collective-permute-start | bytes 1671176 | tf_op jit(solution)/shard_map/ppermute | solution.py:485
  22.5 11.4 %collective-permute-start.6 = (bf16[128,128]{1,0:T(8,128)(2,1)S(1)}, bf16[128,128]{1,0:T(8,128)(2,1)S(1)}, u32[]{:S(2)}, u32[]{:S(2)}) collective-permute-start(bf16[128,128]{1,0:T(8,128)(2,1)S(1)} %get-tuple-element.29), channel_id=1, source_target_pairs={{0,3},{1,0},{2,1},{3,2},{4,7},{5,4},{6,5},{7,6},{8,11},{9,8},{10,9... | collective-permute-start | bytes 98312 | tf_op jit(solution)/shard_map/ppermute | solution.py:471
  27.7 13.5 %collective-permute-start.5 = (bf16[128,128]{1,0:T(8,128)(2,1)S(1)}, bf16[128,128]{1,0:T(8,128)(2,1)S(1)}, u32[]{:S(2)}, u32[]{:S(2)}) collective-permute-start(bf16[128,128]{1,0:T(8,128)(2,1)S(1)} %get-tuple-element.30), channel_id=1, source_target_pairs={{0,2},{1,3},{2,0},{3,1},{4,6},{5,7},{6,4},{7,5},{8,10},{9,11},{10,... | collective-permute-start | bytes 98312 | tf_op jit(solution)/shard_map/ppermute | solution.py:471
  28.8 12.4 %collective-permute-start.4 = (bf16[128,128]{1,0:T(8,128)(2,1)S(1)}, bf16[128,128]{1,0:T(8,128)(2,1)S(1)}, u32[]{:S(2)}, u32[]{:S(2)}) collective-permute-start(bf16[128,128]{1,0:T(8,128)(2,1)S(1)} %get-tuple-element.28), channel_id=1, source_target_pairs={{0,1},{1,2},{2,3},{3,0},{4,5},{5,6},{6,7},{7,4},{8,9},{9,10},{10,1... | collective-permute-start | bytes 98312 | tf_op jit(solution)/shard_map/ppermute | solution.py:471
  30.9 21.4 %collective-permute-start.2 = (bf16[272,1024]{1,0:T(8,128)(2,1)S(1)}, bf16[272,1024]{1,0:T(8,128)(2,1)}, u32[]{:S(2)}, u32[]{:S(2)}) collective-permute-start(bf16[272,1024]{1,0:T(8,128)(2,1)S(1)} %concatenate.33.refs_1_), channel_id=1, source_target_pairs={{0,4},{4,0},{1,5},{5,1},{2,6},{6,2},{3,7},{7,3},{8,12},{12,8},{9,1... | collective-permute-start | bytes 1671176 | tf_op jit(solution)/shard_map/ppermute | solution.py:489
  41.2 11.1 %copy-start.2 = (s32[128]{0:T(128)S(1)}, s32[128]{0:T(128)}, u32[]{:S(2)}) copy-start(s32[128]{0:T(128)} %order_ref.3) | copy-start | bytes 1540
  41.2 11.1 %copy-start.4 = (bf16[272,1024]{1,0:T(8,128)(2,1)}, bf16[272,1024]{1,0:T(8,128)(2,1)S(1)}, u32[]{:S(2)}) copy-start(bf16[272,1024]{1,0:T(8,128)(2,1)S(1)} %collective-permute-done.3.refs_3_) | copy-start | bytes 1671172
  42.6 9.7 %collective-permute-start.7 = (bf16[272,1024]{1,0:T(8,128)(2,1)S(1)}, bf16[272,1024]{1,0:T(8,128)(2,1)}, u32[]{:S(2)}, u32[]{:S(2)}) collective-permute-start(bf16[272,1024]{1,0:T(8,128)(2,1)S(1)} %collective-permute-done.3.refs_3_), channel_id=1, source_target_pairs={{0,4},{4,0},{1,5},{5,1},{2,6},{6,2},{3,7},{7,3},{8,12},{12,8},{9,1... | collective-permute-start | bytes 1671176 | tf_op jit(solution)/shard_map/ppermute | solution.py:491
  45.6 32.3 %all-to-all-start.1 = ((bf16[16,128,384]{2,1,0:T(8,128)(2,1)}), bf16[16,128,384]{2,1,0:T(8,128)(2,1)}, u32[]{:S(2)}, u32[]{:S(2)}) async-start(bf16[16,128,384]{2,1,0:T(8,128)(2,1)} %broadcast_in_dim.17), calls=%async_computation.1 | async-start | bytes 3145728 | tf_op jit(solution)/shard_map/all_to_all | solution.py:497
  52.3 7.6 %copy-start.3 = (s32[4]{0:T(128)}, s32[4]{0:T(128)S(1)}, u32[]{:S(2)}) copy-start(s32[4]{0:T(128)S(1)} %pad_add_fusion.1.place_ref) | copy-start | bytes 52
  59.9 5.4 %copy-start.5 = (f32[16,512]{1,0:T(8,128)}, f32[16,512]{1,0:T(8,128)S(1)}, u32[]{:S(2)}) copy-start(f32[16,512]{1,0:T(8,128)S(1)} %shard_map.86.refs_5_) | copy-start | bytes 98308
  59.9 2.2 %collective-permute-start.8 = (f32[16,512]{1,0:T(8,128)S(1)}, f32[16,512]{1,0:T(8,128)S(1)}, u32[]{:S(2)}, u32[]{:S(2)}) collective-permute-start(f32[16,512]{1,0:T(8,128)S(1)} %shard_map.86.refs_5_), channel_id=1, source_target_pairs={{0,4},{4,0},{1,5},{5,1},{2,6},{6,2},{3,7},{7,3},{8,12},{12,8},{9,1... | collective-permute-start | bytes 98312 | tf_op jit(solution)/shard_map/ppermute | solution.py:504
  60.3 3.2 %collective-permute-start.9 = (f32[16,512]{1,0:T(8,128)S(1)}, f32[16,512]{1,0:T(8,128)S(1)}, u32[]{:S(2)}, u32[]{:S(2)}) collective-permute-start(f32[16,512]{1,0:T(8,128)S(1)} %shard_map.86.refs_5_), channel_id=1, source_target_pairs={{0,32},{32,0},{1,33},{33,1},{2,34},{34,2},{3,35},{35,3},{4,36},{36... | collective-permute-start | bytes 98312 | tf_op jit(solution)/shard_map/ppermute | solution.py:505
  61.4 3.9 %collective-permute-start.10 = (f32[16,512]{1,0:T(8,128)S(1)}, f32[16,512]{1,0:T(8,128)S(1)}, u32[]{:S(2)}, u32[]{:S(2)}) collective-permute-start(f32[16,512]{1,0:T(8,128)S(1)} %shard_map.86.refs_5_), channel_id=1, source_target_pairs={{0,36},{4,32},{32,4},{36,0},{1,37},{5,33},{33,5},{37,1},{2,38},{6,... | collective-permute-start | bytes 98312 | tf_op jit(solution)/shard_map/ppermute | solution.py:506
  62.2 3.1 %copy-start.10 = (f32[16,512]{1,0:T(8,128)}, f32[16,512]{1,0:T(8,128)S(1)}, u32[]{:S(2)}) copy-start(f32[16,512]{1,0:T(8,128)S(1)} %collective-permute-done.8.refs_6_) | copy-start | bytes 98308
  63.5 1.8 %copy-start.11 = (f32[16,512]{1,0:T(8,128)}, f32[16,512]{1,0:T(8,128)S(1)}, u32[]{:S(2)}) copy-start(f32[16,512]{1,0:T(8,128)S(1)} %collective-permute-done.9.refs_7_) | copy-start | bytes 98308
  77.9 46.5 %collective-permute-start.11 = (bf16[2048,384]{1,0:T(8,128)(2,1)}, bf16[2048,384]{1,0:T(8,128)(2,1)}, u32[]{:S(2)}, u32[]{:S(2)}) collective-permute-start(bf16[2048,384]{1,0:T(8,128)(2,1)} %bitcast.23.mine_ref), channel_id=1, source_target_pairs={{0,4},{4,0},{1,5},{5,1},{2,6},{6,2},{3,7},{7,3},{8,12},{12,8},{9,1... | collective-permute-start | bytes 4718600 | tf_op jit(solution)/shard_map/ppermute | solution.py:513
  78.0 24.9 %all-to-all-start.2 = ((bf16[16,128,256]{2,1,0:T(8,128)(2,1)}), bf16[16,128,256]{2,1,0:T(8,128)(2,1)S(1)}, u32[]{:S(2)}, u32[]{:S(2)}) async-start(bf16[16,128,256]{2,1,0:T(8,128)(2,1)} %bitcast.38), calls=%async_computation.2 | async-start | bytes 2097152 | tf_op jit(solution)/shard_map/all_to_all | solution.py:519
  90.0 24.1 %collective-permute-start.14 = (bf16[128,1024]{1,0:T(8,128)(2,1)}, bf16[128,1024]{1,0:T(8,128)(2,1)}, u32[]{:S(2)}, u32[]{:S(2)}) collective-permute-start(bf16[128,1024]{1,0:T(8,128)(2,1)} %get-tuple-element.23), channel_id=1, source_target_pairs={{0,36},{4,32},{32,4},{36,0},{1,37},{5,33},{33,5},{37,1},{2,38},{6,... | collective-permute-start | bytes 786440 | tf_op jit(solution)/shard_map/ppermute | solution.py:546
  91.3 22.8 %collective-permute-start.13 = (bf16[128,1024]{1,0:T(8,128)(2,1)}, bf16[128,1024]{1,0:T(8,128)(2,1)}, u32[]{:S(2)}, u32[]{:S(2)}) collective-permute-start(bf16[128,1024]{1,0:T(8,128)(2,1)} %get-tuple-element.22), channel_id=1, source_target_pairs={{0,32},{32,0},{1,33},{33,1},{2,34},{34,2},{3,35},{35,3},{4,36},{36... | collective-permute-start | bytes 786440 | tf_op jit(solution)/shard_map/ppermute | solution.py:545
  92.1 22.0 %collective-permute-start.12 = (bf16[128,1024]{1,0:T(8,128)(2,1)}, bf16[128,1024]{1,0:T(8,128)(2,1)}, u32[]{:S(2)}, u32[]{:S(2)}) collective-permute-start(bf16[128,1024]{1,0:T(8,128)(2,1)} %get-tuple-element.21), channel_id=1, source_target_pairs={{0,4},{4,0},{1,5},{5,1},{2,6},{6,2},{3,7},{7,3},{8,12},{12,8},{9,1... | collective-permute-start | bytes 786440 | tf_op jit(solution)/shard_map/ppermute | solution.py:544
  104.3 20.0 %all-to-all-start.3 = ((bf16[16,32,256]{2,1,0:T(8,128)(2,1)}), bf16[16,32,256]{2,1,0:T(8,128)(2,1)S(1)}, u32[]{:S(2)}, u32[]{:S(2)}) async-start(bf16[16,32,256]{2,1,0:T(8,128)(2,1)} %shard_map.88), calls=%async_computation.3 | async-start | bytes 524288 | tf_op jit(solution)/shard_map/all_to_all | solution.py:539
  112.7 1.4 %copy-start.7 = (f32[128,1024]{1,0:T(8,128)S(1)}, f32[128,1024]{1,0:T(8,128)}, u32[]{:S(2)}) copy-start(f32[128,1024]{1,0:T(8,128)} %get-tuple-element.20) | copy-start | bytes 1572868
  (1 other events, 0.6 us)
